TPU v7x, 256 devices: a whole 4x4x8 slice. The times are simulated.
256 devices in a mesh: pre: 8 (over z_hi, y), dec: 32 (over x, z_lo, core).
Axes of the slice: x: 4, y: 4, z: 8 (z_hi: 2, z_lo: 4; z = z_hi * 4 + z_lo), core: 2. Of those that a mesh axis runs over, the one named last changes fastest.
Arguments:
- prompt_x: bfloat16 [32768, 4096], P('dec', 'pre'), may hold values from -6 to 6
- w_dkv: bfloat16 [4096, 576], P('pre'), may hold values from -0.09375 to 0.09375
- kv_gain: float32 [512], replicated, may hold values from 0.25 to 1.75
- cache_pool: bfloat16 [1024, 36864], P('dec'), may hold values from -8 to 8
- queries: bfloat16 [256, 73728], P('dec', 'pre'), may hold values from -8 to 8
- row_lengths: int32 [256], P('dec'), may hold values from 1 to 256, as said below
- page_dest: int32 [512], replicated, may hold values from 0 to 31, as said below
- page_slot: int32 [512], replicated, may hold values from 0 to 31, as said below
- moe_x: bfloat16 [2048, 4096], P('dec'), may hold values from -6 to 6
- expert_ids: int32 [2048, 8], P('dec'), may hold values from 0 to 127, all different within a row; in each aligned block of 64 rows (0 to 63, 64 to 127, ...) at most 8 rows name the same one
- expert_weights: bfloat16 [2048, 8], P('dec'), may hold values from 0.099609375 to 1
- w_gate_up: bfloat16 [128, 2, 4096, 1024], P('dec', None, None, 'pre'), may hold values from -0.09375 to 0.09375
Outputs:
- attn_latent: bfloat16 [256, 65536], P('dec', 'pre')
- expert_hidden: bfloat16 [128, 256, 1024], P('dec', None, 'pre')
Inputs may be any that keep to these rules, and one draw needn't show every extreme that they name: `row_lengths`: each decode row has at least one valid position; on every index of dec some row uses all 256 positions. `page_dest`: entry s * 16 + p names the dec index whose pool receives page p of the prompt held on dec index s. The 16 pages of one prompt go to 16 different indices, and one index receives a page of every prompt. `page_slot`: the page's row among the 32 rows of the receiving pool; no two pages that reach one index of dec share a row. `expert_ids`: each row names 8 different experts. In the rows of one index of dec (aligned blocks of 64 rows) no expert is named by more than 8 rows.
All inputs are finite; a program needn't handle non-finite values.
Results may differ from a plain program's by a relative error of at most 0.0059.
Values may be sent and summed in bfloat16 or wider, within the bound.
A program may use at most 128 MiB of HBM per device.

v0:
```python
import jax
import jax.numpy as jnp
from jax import lax
from jax.sharding import PartitionSpec as P

KVL = 512
LAT = 576
HEAD_QK = 192
PAGE = 64
EXP_DEV = 4
P_TOK = 1024
R_ATT = 8
PAGES_ROW = 4
R_MOE = 64
PP = 16
SLOTS = 32


NORM_EPSILON = 1e-06


def rotate_cache(latent, gain_vec, position):
    kv_count = gain_vec.shape[0]
    lat_part = latent[:, :kv_count]
    rope_part = latent[:, kv_count:]
    normed = (
        lat_part
        * lax.rsqrt(jnp.mean(lat_part * lat_part, axis=1, keepdims=True) + NORM_EPSILON)
        * gain_vec
    )
    halfway = rope_part.shape[1] // 2
    frequency = 10000.0 ** (-2.0 * jnp.arange(halfway, dtype=jnp.float32) / (2 * halfway))
    angles = position.astype(jnp.float32)[:, None] * frequency[None, :]
    lead_half = rope_part[:, :halfway]
    tail_half = rope_part[:, halfway:]
    cosine = jnp.cos(angles)
    sine_vals = jnp.sin(angles)
    rotated = jnp.concatenate(
        [lead_half * cosine - tail_half * sine_vals, tail_half * cosine + lead_half * sine_vals],
        axis=1,
    )
    return jnp.concatenate([normed, rotated], axis=1).astype(jnp.bfloat16)


def shards(
    prompt_x,
    w_dkv,
    kv_gain,
    cache_pool,
    queries,
    row_lengths,
    page_dest,
    page_slot,
    moe_x,
    expert_ids,
    expert_weights,
    w_gate_up,
):
    n_dec = lax.axis_size("dec")
    dec_index = lax.axis_index("dec")
    dest_table = page_dest.reshape(n_dec, PP)
    slot_table = page_slot.reshape(n_dec, PP)
    my_dest = lax.dynamic_index_in_dim(dest_table, dec_index, 0, keepdims=False)
    select = (my_dest[None, :] == jnp.arange(n_dec, dtype=jnp.int32)[:, None]).astype(jnp.bfloat16)
    partial_sum = jnp.dot(prompt_x, w_dkv, preferred_element_type=jnp.float32)
    latent_total = lax.psum(partial_sum, "pre")
    positions = jnp.arange(P_TOK, dtype=jnp.int32)
    prompt_cache = rotate_cache(latent_total, kv_gain, positions)
    page_rows = prompt_cache.reshape(PP, PAGE * LAT)
    outgoing = jnp.dot(select, page_rows, preferred_element_type=jnp.float32).astype(jnp.bfloat16)
    arrived = lax.all_to_all(outgoing, "dec", split_axis=0, concat_axis=0, tiled=True)
    hit_page = dest_table == dec_index
    from_source = jnp.any(hit_page, axis=1)
    source_slot = jnp.sum(jnp.where(hit_page, slot_table, 0), axis=1)
    placing = (source_slot[None, :] == jnp.arange(SLOTS, dtype=jnp.int32)[:, None]) & from_source[
        None, :
    ]
    landed = jnp.dot(
        placing.astype(jnp.bfloat16), arrived, preferred_element_type=jnp.float32
    ).astype(jnp.bfloat16)
    new_pool = jnp.where(jnp.any(placing, axis=1)[:, None], landed, cache_pool)
    kv_rows = new_pool.reshape(R_ATT, PAGES_ROW * PAGE, LAT)
    heads_here = queries.shape[1] // LAT
    query_view = queries.reshape(R_ATT, heads_here, LAT)
    scores = jnp.einsum(
        "rhc,rtc->rht", query_view, kv_rows, preferred_element_type=jnp.float32
    ) * HEAD_QK ** (-0.5)
    in_length = (
        jnp.arange(PAGES_ROW * PAGE, dtype=jnp.int32)[None, None, :] < row_lengths[:, None, None]
    )
    masked = jnp.where(in_length, scores, -jnp.inf)
    top_score = jnp.max(masked, axis=2, keepdims=True)
    weights_raw = jnp.exp(masked - top_score)
    attn_probs = (weights_raw / jnp.sum(weights_raw, axis=2, keepdims=True)).astype(jnp.bfloat16)
    attn_sum = jnp.einsum(
        "rht,rtc->rhc", attn_probs, kv_rows[:, :, :KVL], preferred_element_type=jnp.float32
    )
    attn_latent = attn_sum.astype(jnp.bfloat16).reshape(R_ATT, heads_here * KVL)
    experts_all = EXP_DEV * n_dec
    capacity = 16 * R_MOE // experts_all
    expert_axis = jnp.arange(experts_all, dtype=jnp.int32)
    matches = expert_ids[:, :, None] == expert_axis[None, None, :]
    member = jnp.any(matches, axis=1)
    row_weight = jnp.sum(
        jnp.where(matches, expert_weights[:, :, None].astype(jnp.float32), 0.0), axis=1
    )
    member_int = member.astype(jnp.int32)
    row_rank = jnp.cumsum(member_int, axis=0) - member_int
    hit_slot = member[:, :, None] & (
        row_rank[:, :, None] == jnp.arange(capacity, dtype=jnp.int32)[None, None, :]
    )
    slot_filled = jnp.any(hit_slot, axis=0)
    slot_row = jnp.sum(
        jnp.where(hit_slot, jnp.arange(R_MOE, dtype=jnp.int32)[:, None, None], 0), axis=0
    )
    slot_weight = jnp.sum(jnp.where(hit_slot, row_weight[:, :, None], 0.0), axis=0).astype(
        jnp.bfloat16
    )
    weight_out = slot_weight.reshape(n_dec, EXP_DEV, capacity)
    sent_rows = jnp.where(slot_filled[:, :, None], jnp.take(moe_x, slot_row, axis=0), 0)
    outbound = sent_rows.reshape(n_dec, EXP_DEV, capacity, moe_x.shape[1])
    inbound, inbound_weight = (
        lax.all_to_all(outbound, "dec", split_axis=0, concat_axis=0, tiled=True),
        lax.all_to_all(weight_out, "dec", split_axis=0, concat_axis=0, tiled=True),
    )
    gate_up = jnp.einsum("secd,etdf->tescf", inbound, w_gate_up, preferred_element_type=jnp.float32)
    slot_scale = jnp.transpose(inbound_weight, (1, 0, 2))[:, :, :, None].astype(jnp.float32)
    hidden = jax.nn.silu(gate_up[0]) * gate_up[1] * slot_scale
    expert_hidden = hidden.astype(jnp.bfloat16).reshape(
        EXP_DEV, n_dec * capacity, w_gate_up.shape[3]
    )
    return (attn_latent, expert_hidden)


def solution(mesh):
    return jax.shard_map(
        shards,
        mesh=mesh,
        in_specs=(
            P("dec", "pre"),
            P("pre", None),
            P(),
            P("dec", None),
            P("dec", "pre"),
            P("dec"),
            P(),
            P(),
            P("dec", None),
            P("dec", None),
            P("dec", None),
            P("dec", None, None, "pre"),
        ),
        out_specs=(P("dec", "pre"), P("dec", None, "pre")),
        check_vma=False,
    )
```

profile of v0, /device:TPU:1, one launch (start us, length us, event | category | flops | bytes accessed | tf_op | source)
XLA Modules:
  0.0 437.7 jit_solution(4696228719909105357)
XLA Ops:
  7.2 1.2 copy-done
  8.4 3.3 fusion.48
  11.7 0.7 copy-done.9
  12.3 0.1 copy.42
  12.4 0.2 fusion.28
  12.6 0.1 copy.47
  12.7 0.1 reduce_window_sum.11
  12.8 0.2 select_reduce_fusion.1
  13.0 0.1 select_reduce_fusion
  13.1 0.7 copy.48
  13.9 10.1 %all-to-all-start.2 = ((bf16[32,4,8]{2,1,0:T(4,128)(2,1)}), bf16[32,4,8]{2,1,0:T(4,128)(2,1)}, u32[]{:S(2)}, u32[]{:S(2)}) async-start(bf16[32,4,8]{2,1,0:T(4,128)(2,1)} %bitcast.13), calls=%async_computation.2 | async-start | bytes 65536 | tf_op jit(solution)/shard_map/all_to_all | solution.py:124
  23.9 0.1 reshape.121
  24.1 130.1 %all-reduce.2.cloned.1.call-done = f32[1024,576]{0,1:T(8,128)} async-done(((f32[1024,576]{0,1:T(8,128)}), f32[1024,576]{0,1:T(8,128)}) %all-reduce.2.cloned.1.call-update) | async-done | bytes 2359312 | tf_op jit(solution)/shard_map/psum | solution.py:66
  154.1 1.9 multiply_reduce_fusion
  156.1 1.5 fusion.36
  157.6 0.2 multiply_convert_fusion
  157.9 0.1 pad_maximum_fusion
  158.0 0.7 copy.39
  158.7 2.4 convert_element_type.66
  161.1 2.0 fusion.2
  163.1 0.5 broadcast.91
  163.6 3.1 reduce
  166.7 4.7 %reshape.139 = bf16[32,2,18432]{2,1,0:T(2,128)(2,1)} reshape(bf16[32,36864]{1,0:T(8,128)(2,1)} %reduce) | data formatting | bytes 4718592
  171.4 5.0 %all-to-all-start = ((bf16[32,2,18432]{2,1,0:T(2,128)(2,1)}), bf16[32,2,18432]{2,1,0:T(2,128)(2,1)S(1)}, u32[]{:S(2)}, u32[]{:S(2)}) async-start(bf16[32,2,18432]{2,1,0:T(2,128)(2,1)} %reshape.139), calls=%async_computation | async-start | bytes 4718592 | tf_op jit(solution)/shard_map/all_to_all | solution.py:71
  176.5 0.1 copy.43
  176.7 0.1 copy.44
  176.8 0.1 copy.45
  176.9 0.1 reshape.129
  177.0 7.8 %gather_fusion = bf16[1024,4096]{1,0:T(8,128)(2,1)} fusion(bf16[64,4096]{1,0:T(8,128)(2,1)S(1)} %copy-done.2, s32[1024]{0:T(1024)S(1)} %broadcast_clamp_fusion), kind=kCustom, calls=%fused_computation | custom fusion | bytes 16781312 | tf_op jit(solution)/shard_map/jit(_take)/gather | solution.py:120
  184.9 7.4 %select_select_fusion = bf16[32,4,8,4096]{3,2,1,0:T(8,128)(2,1)} fusion(bf16[32,4,8,4096]{3,2,1,0:T(8,128)(2,1)} %bitcast.54, pred[32,4,8]{2,1,0:T(4,128)(4,1)S(1)} %compare_and_fusion, pred[32,4,8]{2,1,0:T(4,128)(4,1)S(1)} %bitcast.57), kind=kLoop, calls=%fused_computation.9 | loop fusion | flops 8388608 | bytes 16779264 | tf_op jit(solution)/shard_map/jit(_where)/select_n | solution.py:120
  192.3 39.3 %all-to-all-done = bf16[32,2,18432]{2,1,0:T(2,128)(2,1)S(1)} async-done(((bf16[32,2,18432]{2,1,0:T(2,128)(2,1)}), bf16[32,2,18432]{2,1,0:T(2,128)(2,1)S(1)}, u32[]{:S(2)}, u32[]{:S(2)}) %all-to-all-start) | async-done | bytes 2359328 | tf_op jit(solution)/shard_map/all_to_all | solution.py:71
  231.6 5.6 %all-to-all-start.1 = ((bf16[32,4,8,4096]{3,2,1,0:T(8,128)(2,1)}), bf16[32,4,8,4096]{3,2,1,0:T(8,128)(2,1)}, u32[]{:S(2)}, u32[]{:S(2)}) async-start(bf16[32,4,8,4096]{3,2,1,0:T(8,128)(2,1)} %select_select_fusion), calls=%async_computation.1 | async-start | bytes 16777216 | tf_op jit(solution)/shard_map/all_to_all | solution.py:123
  237.3 0.1 reshape.122
  237.4 0.2 reshape.124
  237.6 0.1 fusion.46
  237.7 0.1 select_reduce_fusion.3
  237.8 0.1 fusion.42
  238.0 0.8 convert_bitcast_fusion
  238.8 0.1 reshape.126
  238.9 7.0 %reshape.140 = bf16[32,1,36864]{2,1,0:T(2,128)(2,1)} reshape(bf16[32,2,18432]{2,1,0:T(2,128)(2,1)S(1)} %all-to-all-done) | data formatting | bytes 4718592
  245.9 6.3 %fusion.1 = bf16[32,36864]{1,0:T(8,128)(2,1)S(1)} fusion(bf16[32,36864]{1,0:T(8,128)(2,1)} %param.15, bf16[32,1,36864]{2,1,0:T(2,128)(2,1)} %reshape.140, pred[32]{0:T(512)(128)(4,1)S(1)} %fusion.42, s32[32]{0:T(128)S(1)} %select_reduce_fusion.3, pred[32]{0:T(512)(128)(4,1)S(1)} %get-tuple-element.2), kind=kOutput, calls=%fused_computation.4 | convolution fusion | flops 77858816 | bytes 7078080 | tf_op jit(solution)/shard_map/dot_general | solution.py:78
  252.2 4.1 reshape.123
  256.3 2.7 fusion.47
  259.0 2.0 fusion.22
  261.0 0.8 copy.56
  261.8 159.9 %all-to-all-done.1 = bf16[32,4,8,4096]{3,2,1,0:T(8,128)(2,1)} async-done(((bf16[32,4,8,4096]{3,2,1,0:T(8,128)(2,1)}), bf16[32,4,8,4096]{3,2,1,0:T(8,128)(2,1)}, u32[]{:S(2)}, u32[]{:S(2)}) %all-to-all-start.1) | async-done | bytes 8388640 | tf_op jit(solution)/shard_map/all_to_all | solution.py:123
  421.7 8.2 %fusion.10 = f32[2,4,32,8,128]{4,3,0,2,1:T(8,128)S(1)} fusion(bf16[4,2,4096,128]{3,2,1,0:T(8,128)(2,1)} %param.23, bf16[32,4,8,4096]{3,2,1,0:T(8,128)(2,1)} %all-to-all-done.1), kind=kOutput, calls=%fused_computation.16 | convolution fusion | flops 2147483648 | bytes 17825792 | tf_op jit(solution)/shard_map/secd,etdf->tescf/dot_general | solution.py:126
  429.9 0.9 fusion.27
  (44 shorter events, 0.4 us)
Async XLA Ops:
  7.2 1.2 copy-start
  7.2 146.9 %all-reduce.2.cloned.1.call-start = ((), (), s32[]{:S(2)}) async-start(), calls=%async_computation.3 | async-start | bytes 4718592 | tf_op jit(solution)/shard_map/psum | solution.py:66
  11.7 0.7 copy-start.9
  11.7 1.0 copy-start.10
  11.7 12.3 %copy-start.11 = (s32[512]{0:T(512)S(1)}, s32[512]{0:T(512)}, u32[]{:S(2)}) copy-start(s32[512]{0:T(512)} %param.18) | copy-start | bytes 6148
  11.7 146.0 %copy-start.13 = (f32[512]{0:T(512)S(1)}, f32[512]{0:T(512)}, u32[]{:S(2)}) copy-start(f32[512]{0:T(512)} %param.14) | copy-start | bytes 6148
  13.0 143.0 %copy-start.4 = (s32[64,128]{1,0:T(8,128)}, s32[64,128]{1,0:T(8,128)S(1)}, u32[]{:S(2)}) copy-start(s32[64,128]{1,0:T(8,128)S(1)} %convert_subtract_fusion) | copy-start | bytes 98308
  13.9 157.5 %all-to-all-start.2 = ((bf16[32,4,8]{2,1,0:T(4,128)(2,1)}), bf16[32,4,8]{2,1,0:T(4,128)(2,1)}, u32[]{:S(2)}, u32[]{:S(2)}) async-start(bf16[32,4,8]{2,1,0:T(4,128)(2,1)} %bitcast.13), calls=%async_computation.2 | async-start | bytes 65536 | tf_op jit(solution)/shard_map/all_to_all | solution.py:124
  24.0 132.0 %copy-start.7 = (s32[32,16]{1,0:T(8,128)}, s32[32,16]{1,0:T(8,128)S(1)}, u32[]{:S(2)}) copy-start(s32[32,16]{1,0:T(8,128)S(1)} %reshape.121) | copy-start | bytes 6148
  154.1 3.5 copy-start.3
  171.4 5.0 %copy-start.5 = (s32[64,128]{1,0:T(8,128)S(1)}, s32[64,128]{1,0:T(8,128)}, u32[]{:S(2)}) copy-start(s32[64,128]{1,0:T(8,128)} %copy-done.4) | copy-start | bytes 98308
  171.4 5.6 %copy-start.2 = (bf16[64,4096]{1,0:T(8,128)(2,1)S(1)}, bf16[64,4096]{1,0:T(8,128)(2,1)}, u32[]{:S(2)}) copy-start(bf16[64,4096]{1,0:T(8,128)(2,1)} %param.20) | copy-start | bytes 1572868
  171.4 60.2 %all-to-all-start = ((bf16[32,2,18432]{2,1,0:T(2,128)(2,1)}), bf16[32,2,18432]{2,1,0:T(2,128)(2,1)S(1)}, u32[]{:S(2)}, u32[]{:S(2)}) async-start(bf16[32,2,18432]{2,1,0:T(2,128)(2,1)} %reshape.139), calls=%async_computation | async-start | bytes 4718592 | tf_op jit(solution)/shard_map/all_to_all | solution.py:71
  192.3 45.0 %copy-start.12 = (s32[512]{0:T(512)S(1)}, s32[512]{0:T(512)}, u32[]{:S(2)}) copy-start(s32[512]{0:T(512)} %param.19) | copy-start | bytes 6148
  192.3 45.1 %copy-start.6 = (bf16[8,9216]{1,0:T(8,128)(2,1)S(1)}, bf16[8,9216]{1,0:T(8,128)(2,1)}, u32[]{:S(2)}) copy-start(bf16[8,9216]{1,0:T(8,128)(2,1)} %param.16) | copy-start | bytes 442372
  192.3 45.2 %copy-start.8 = (s32[32,16]{1,0:T(8,128)S(1)}, s32[32,16]{1,0:T(8,128)}, u32[]{:S(2)}) copy-start(s32[32,16]{1,0:T(8,128)} %copy-done.7) | copy-start | bytes 6148
  192.3 45.6 %copy-start.14 = (s32[8]{0:T(128)S(1)}, s32[8]{0:T(128)}, u32[]{:S(2)}) copy-start(s32[8]{0:T(128)} %param.17) | copy-start | bytes 100
  231.6 190.1 %all-to-all-start.1 = ((bf16[32,4,8,4096]{3,2,1,0:T(8,128)(2,1)}), bf16[32,4,8,4096]{3,2,1,0:T(8,128)(2,1)}, u32[]{:S(2)}, u32[]{:S(2)}) async-start(bf16[32,4,8,4096]{3,2,1,0:T(8,128)(2,1)} %select_select_fusion), calls=%async_computation.1 | async-start | bytes 16777216 | tf_op jit(solution)/shard_map/all_to_all | solution.py:123
  421.7 9.1 %copy-start.1 = (bf16[1024,512]{1,0:T(8,128)(2,1)S(1)}, bf16[1024,512]{1,0:T(8,128)(2,1)}, u32[]{:S(2)}) copy-start(bf16[1024,512]{1,0:T(8,128)(2,1)} %param.12) | copy-start | bytes 3145732
Sparse Core Ops, SparseCore 0:
  11.8 142.2 all-reduce.1
where the time goes:
time: 441 us; the launch traced here: 438 us
  waiting for transfers between devices  329 us (75%)
  local copies, waits for them, and re-layouts  31.7 us (7%)
  matrix products  24.5 us (6%)
  starting transfers between devices  20.8 us (5%)
  other arithmetic  17.1 us (4%)
  between operations  14.3 us (3%)
    all_to_all x1, waiting for transfers between devices, shards(): lax.all_to_all(outbound, 'dec', split_axis=0, concat_axis=0, tiled=True)  160 us
    psum x1, waiting for transfers between devices, shards(): latent_total = lax.psum(partial_sum, 'pre')  130 us
    all_to_all x1, waiting for transfers between devices, shards(): lax.all_to_all(outgoing, 'dec', split_axis=0, concat_axis=0, tiled=True)  39.3 us
    unnamed x34, local copies, waits for them, and re-layouts  14.4 us
    all_to_all x1, starting transfers between devices, shards(): lax.all_to_all(weight_out, 'dec', split_axis=0, concat_axis=0, tiled=True)  10.1 us
  transfers between devices with their start and end apart: 4, of which 3 were waited for; matrix products, arithmetic and copies ran while one was open for 13% of the time, Pallas kernels for 0%

commit v1 on v0

--- a/solution.py
+++ b/solution.py
@@ -1,6 +1,8 @@
 import jax
 import jax.numpy as jnp
 from jax import lax
+from jax.experimental import pallas as pl
+from jax.experimental.pallas import tpu as pltpu
 from jax.sharding import PartitionSpec as P
 
 KVL = 512
@@ -14,9 +16,217 @@
 R_MOE = 64
 PP = 16
 SLOTS = 32
-
-
 NORM_EPSILON = 1e-06
+
+MESH = pl.DeviceIdType.MESH
+A0, A1, B0, B1 = 0, 1, 2, 3
+LEFT = [(-1, 0, A0), (-1, 0, A1), (-1, 0, B0), (-1, 0, B1), (2, 0, A0), (2, 0, B0), (-1, -1, B0), (-1, -1, B1),
+        (-1, 1, B0), (-1, 1, B1), (-1, 2, B0), (-1, 2, B1), (2, -1, B0), (2, 1, B0), (2, 2, B0)]
+RIGHT = [(1, 0, A1), (1, 0, A0), (1, 0, B1), (1, 0, B0), (2, 0, A1), (2, 0, B1), (1, -1, B1), (1, -1, B0),
+         (1, 1, B1), (1, 1, B0), (1, 2, B1), (1, 2, B0), (2, -1, B1), (2, 1, B1), (2, 2, B1)]
+BELOW = [(0, -1, B0), (0, -1, B1), (0, -1, A0), (0, -1, A1), (0, 2, B0), (0, 2, A0), (-1, -1, A0), (-1, -1, A1),
+         (1, -1, A0), (1, -1, A1), (2, -1, A0), (2, -1, A1), (-1, 2, A0), (1, 2, A0), (2, 2, A0)]
+ABOVE = [(0, 1, B1), (0, 1, B0), (0, 1, A1), (0, 1, A0), (0, 2, B1), (0, 2, A1), (-1, 1, A1), (-1, 1, A0),
+         (1, 1, A1), (1, 1, A0), (2, 1, A1), (2, 1, A0), (-1, 2, A1), (1, 2, A1), (2, 2, A1)]
+PASSES = {
+    4: [[(0, 0), (-1, 0)]],
+    5: [[(1, 0), (0, -1)]],
+    6: [[(0, 1), (2, 0)]],
+    8: [[(0, 2), (-1, -1)]],
+    10: [[(1, -1), (-1, 1)]],
+    11: [[(1, 1)]],
+    13: [[(2, -1), (-1, 2)]],
+    14: [[(2, 1), (1, 2)]],
+    15: [[(2, 2)]],
+}
+
+
+def forwards(side, dx, dz, q):
+    if side == "left":
+        on = [(1, 0)] if dx == -1 and q in (A0, B0) else []
+        return on + ([(0, 1), (0, -1)] if q in (A0, A1) else [])
+    if side == "right":
+        on = [(-1, 0)] if dx == 1 and q in (A1, B1) else []
+        return on + ([(0, 1), (0, -1)] if q in (A0, A1) else [])
+    if side == "below":
+        on = [(0, 1)] if dz == -1 and q in (A0, B0) else []
+        return on + ([(1, 0), (-1, 0)] if q in (B0, B1) else [])
+    on = [(0, -1)] if dz == 1 and q in (A1, B1) else []
+    return on + ([(1, 0), (-1, 0)] if q in (B0, B1) else [])
+
+
+def device(x, y, z, c):
+    return (lax.div(z, 4) * 4 + y, (x * 4 + lax.rem(z, 4)) * 2 + c)
+
+
+def expert_kernel(moe_hbm, tag_ref, w_hbm, out_ref, rows, tags, wbuf, slot_ref, wt_ref,
+                  load_sem, w_sem, ici_sem, pair_sem, recv_sem, recv2_sem, tag_send, tag_recv):
+    pre, dec = lax.axis_index("pre"), lax.axis_index("dec")
+    y = lax.rem(pre, 4)
+    c = lax.rem(dec, 2)
+    zl = lax.rem(lax.div(dec, 2), 4)
+    x = lax.div(dec, 8)
+    z = lax.div(pre, 4) * 4 + zl
+    features = rows.shape[2]
+    quarter = features // 4
+
+    def chip(dx, dz):
+        return lax.rem(x + dx + 4, 4) * 4 + lax.rem(z + dz + 8, 4)
+
+    def peer(dx, dz, core):
+        return device(lax.rem(x + dx + 4, 4), y, lax.rem(z + dz + 8, 8), core)
+
+    loads = []
+    for e in range(EXP_DEV):
+        for t in range(2):
+            load = pltpu.make_async_copy(w_hbm.at[e, t], wbuf.at[e, :, pl.ds(t * 128, 128)], w_sem.at[e * 2 + t])
+            load.start()
+            loads.append(load)
+    own = pltpu.make_async_copy(moe_hbm, rows.at[dec], load_sem)
+    own.start()
+    tags[dec] = tag_ref[...]
+
+    barrier = pltpu.get_barrier_semaphore()
+    greeted = 0
+    for dx in (0, 1, 2, 3):
+        for dz in (-2, -1, 0, 1, 2):
+            for dc in (0, 1):
+                if (dx, dz, dc) != (0, 0, 0):
+                    pl.semaphore_signal(barrier, inc=1, device_id=peer(dx, dz, lax.rem(c + dc, 2)), device_id_type=MESH)
+                    greeted += 1
+    pl.semaphore_wait(barrier, greeted)
+
+    def piece(dx, dz, q, core):
+        return rows.at[2 * chip(dx, dz) + core, :, pl.ds(q * quarter, quarter)]
+
+    def push(dx, dz, q, sx, sz):
+        pltpu.make_async_remote_copy(
+            src_ref=piece(dx, dz, q, c), dst_ref=piece(dx, dz, q, c), send_sem=ici_sem,
+            recv_sem=recv_sem.at[chip(dx, dz), q], device_id=peer(sx, sz, c), device_id_type=MESH).start()
+
+    def share(dx, dz, q):
+        pltpu.make_async_remote_copy(
+            src_ref=piece(dx, dz, q, c), dst_ref=piece(dx, dz, q, c), send_sem=pair_sem,
+            recv_sem=recv2_sem.at[chip(dx, dz), q], device_id=peer(0, 0, 1 - c), device_id_type=MESH).start()
+
+    own.wait()
+    for q in (A0, B0, A1, B1):
+        push(0, 0, q, 1, 0)
+        push(0, 0, (q + 2) % 4, 0, 1)
+        push(0, 0, q ^ 1, -1, 0)
+        push(0, 0, (q + 2) % 4 ^ 1, 0, -1)
+    for q in range(4):
+        share(0, 0, q)
+    tag_copies = []
+    for dx in (0, 1, 2, 3):
+        for dz in (-1, 0, 1, 2):
+            for dc in (0, 1):
+                if (dx, dz, dc) != (0, 0, 0):
+                    copy = pltpu.make_async_remote_copy(
+                        src_ref=tag_ref, dst_ref=tags.at[dec], send_sem=tag_send.at[len(tag_copies)], recv_sem=tag_recv.at[dec],
+                        device_id=peer(dx, dz, lax.rem(c + dc, 2)), device_id_type=MESH)
+                    copy.start()
+                    tag_copies.append(copy)
+
+    def read_tags():
+        for dx in (0, 1, 2, 3):
+            for dz in (-1, 0, 1, 2):
+                for dc in (0, 1):
+                    if (dx, dz, dc) != (0, 0, 0):
+                        s = 2 * chip(dx, dz) + lax.rem(c + dc, 2)
+                        pltpu.make_async_copy(tags.at[s], tags.at[s], tag_recv.at[s]).wait()
+        both = tags[...].astype(jnp.float32).reshape(16, 2, 16, 128)
+        both = both[:, 0] + both[:, 1]
+        ids, weights = both[:, :8], both[:, 8:]
+        i0 = lax.broadcasted_iota(jnp.int32, (128, 128), 0)
+        i1 = lax.broadcasted_iota(jnp.int32, (128, 128), 1)
+        earlier = ((i0 < i1) & (lax.div(i0, 64) == lax.div(i1, 64))).astype(jnp.float32).astype(jnp.bfloat16)
+        shift = jnp.where(lax.broadcasted_iota(jnp.int32, (16, 128), 1) >= 64, 8.0, 0.0)
+        for e in range(EXP_DEV):
+            hit = ids == (dec * EXP_DEV + e).astype(jnp.float32)
+            member = jnp.sum(jnp.where(hit, 1.0, 0.0), axis=1)
+            wt_ref[e] = jnp.sum(jnp.where(hit, weights, 0.0), axis=1)
+            rank = jnp.dot(member.astype(jnp.bfloat16), earlier, preferred_element_type=jnp.float32)
+            slot_ref[e] = jnp.where(member > 0.5, rank + shift, -1.0)
+
+    def wait_item(dx, dz):
+        for q in range(4):
+            other = piece(dx, dz, q, 1 - c)
+            pltpu.make_async_copy(other, other, recv2_sem.at[chip(dx, dz), q]).wait()
+
+    def experts(items):
+        blocks = [rows[pl.ds(2 * chip(dx, dz), 2)].reshape(128, features) for dx, dz in items]
+        lhs = blocks[0] if len(blocks) == 1 else jnp.concatenate(blocks, axis=0)
+        i0 = lax.broadcasted_iota(jnp.int32, (128, 128), 0)
+        i1 = lax.broadcasted_iota(jnp.int32, (128, 128), 1)
+        place = lax.broadcasted_iota(jnp.int32, (16, 128), 0).astype(jnp.float32)
+        for e in range(EXP_DEV):
+            both = jnp.dot(lhs, wbuf[e], preferred_element_type=jnp.float32)
+            for n, (dx, dz) in enumerate(items):
+                k = chip(dx, dz)
+                gate, up = both[n * 128:(n + 1) * 128, :128], both[n * 128:(n + 1) * 128, 128:]
+                wrow = wt_ref[e, pl.ds(k, 1), :]
+                spread = jnp.where(i0 == i1, jnp.broadcast_to(wrow, (128, 128)), 0.0).astype(jnp.bfloat16)
+                wcol = jnp.dot(spread, jnp.ones((128, 128), jnp.bfloat16), preferred_element_type=jnp.float32)
+                hidden = (gate / (1.0 + jnp.exp(-gate)) * up * wcol).astype(jnp.bfloat16)
+                srow = slot_ref[e, pl.ds(k, 1), :]
+                choose = jnp.where(jnp.broadcast_to(srow, (16, 128)) == place, 1.0, 0.0).astype(jnp.bfloat16)
+                out_ref[e, pl.ds(pl.multiple_of(k * 16, 16), 16), :] = jnp.dot(
+                    choose, hidden, preferred_element_type=jnp.float32).astype(jnp.bfloat16)
+
+    for n in range(1, 16):
+        for side, plan in (("left", LEFT), ("right", RIGHT), ("below", BELOW), ("above", ABOVE)):
+            dx, dz, q = plan[n - 1]
+            got = piece(dx, dz, q, c)
+            pltpu.make_async_copy(got, got, recv_sem.at[chip(dx, dz), q]).wait()
+            for sx, sz in forwards(side, dx, dz, q):
+                push(dx, dz, q, sx, sz)
+            share(dx, dz, q)
+        if n == 1:
+            read_tags()
+            for load in loads:
+                load.wait()
+        for items in PASSES.get(n, []):
+            for dx, dz in items:
+                wait_item(dx, dz)
+            experts(items)
+
+    sent = rows.at[pl.ds(0, 15)]
+    pltpu.make_async_copy(sent, sent, ici_sem).wait()
+    sent = rows.at[pl.ds(0, 16)]
+    pltpu.make_async_copy(sent, sent, pair_sem).wait()
+    for copy in tag_copies:
+        copy.wait_send()
+
+
+def expert_part(moe_x, expert_ids, expert_weights, w_gate_up):
+    c = lax.rem(lax.axis_index("dec"), 2)
+    tag = jnp.concatenate([expert_ids.T.astype(jnp.bfloat16), expert_weights.T], axis=0)
+    zero = jnp.zeros_like(tag)
+    tag = jnp.where(c == 0, jnp.concatenate([tag, zero], axis=1), jnp.concatenate([zero, tag], axis=1))
+    features = moe_x.shape[1]
+    return pl.pallas_call(
+        expert_kernel,
+        out_shape=jax.ShapeDtypeStruct((EXP_DEV, 256, 128), jnp.bfloat16),
+        in_specs=[pl.BlockSpec(memory_space=pl.ANY), pl.BlockSpec(memory_space=pltpu.VMEM), pl.BlockSpec(memory_space=pl.ANY)],
+        out_specs=pl.BlockSpec(memory_space=pltpu.VMEM),
+        scratch_shapes=[
+            pltpu.VMEM((32, R_MOE, features), jnp.bfloat16),
+            pltpu.VMEM((32, 16, 128), jnp.bfloat16),
+            pltpu.VMEM((EXP_DEV, features, 256), jnp.bfloat16),
+            pltpu.VMEM((EXP_DEV, 16, 128), jnp.float32),
+            pltpu.VMEM((EXP_DEV, 16, 128), jnp.float32),
+            pltpu.SemaphoreType.DMA,
+            pltpu.SemaphoreType.DMA((8,)),
+            pltpu.SemaphoreType.DMA,
+            pltpu.SemaphoreType.DMA,
+            pltpu.SemaphoreType.DMA((16, 4)),
+            pltpu.SemaphoreType.DMA((16, 4)),
+            pltpu.SemaphoreType.DMA((31,)),
+            pltpu.SemaphoreType.DMA((32,)),
+        ],
+        compiler_params=pltpu.CompilerParams(collective_id=0, has_side_effects=True, vmem_limit_bytes=56 * 1024 * 1024),
+    )(moe_x, tag, w_gate_up)
 
 
 def rotate_cache(latent, gain_vec, position):
@@ -96,39 +306,7 @@
         "rht,rtc->rhc", attn_probs, kv_rows[:, :, :KVL], preferred_element_type=jnp.float32
     )
     attn_latent = attn_sum.astype(jnp.bfloat16).reshape(R_ATT, heads_here * KVL)
-    experts_all = EXP_DEV * n_dec
-    capacity = 16 * R_MOE // experts_all
-    expert_axis = jnp.arange(experts_all, dtype=jnp.int32)
-    matches = expert_ids[:, :, None] == expert_axis[None, None, :]
-    member = jnp.any(matches, axis=1)
-    row_weight = jnp.sum(
-        jnp.where(matches, expert_weights[:, :, None].astype(jnp.float32), 0.0), axis=1
-    )
-    member_int = member.astype(jnp.int32)
-    row_rank = jnp.cumsum(member_int, axis=0) - member_int
-    hit_slot = member[:, :, None] & (
-        row_rank[:, :, None] == jnp.arange(capacity, dtype=jnp.int32)[None, None, :]
-    )
-    slot_filled = jnp.any(hit_slot, axis=0)
-    slot_row = jnp.sum(
-        jnp.where(hit_slot, jnp.arange(R_MOE, dtype=jnp.int32)[:, None, None], 0), axis=0
-    )
-    slot_weight = jnp.sum(jnp.where(hit_slot, row_weight[:, :, None], 0.0), axis=0).astype(
-        jnp.bfloat16
-    )
-    weight_out = slot_weight.reshape(n_dec, EXP_DEV, capacity)
-    sent_rows = jnp.where(slot_filled[:, :, None], jnp.take(moe_x, slot_row, axis=0), 0)
-    outbound = sent_rows.reshape(n_dec, EXP_DEV, capacity, moe_x.shape[1])
-    inbound, inbound_weight = (
-        lax.all_to_all(outbound, "dec", split_axis=0, concat_axis=0, tiled=True),
-        lax.all_to_all(weight_out, "dec", split_axis=0, concat_axis=0, tiled=True),
-    )
-    gate_up = jnp.einsum("secd,etdf->tescf", inbound, w_gate_up, preferred_element_type=jnp.float32)
-    slot_scale = jnp.transpose(inbound_weight, (1, 0, 2))[:, :, :, None].astype(jnp.float32)
-    hidden = jax.nn.silu(gate_up[0]) * gate_up[1] * slot_scale
-    expert_hidden = hidden.astype(jnp.bfloat16).reshape(
-        EXP_DEV, n_dec * capacity, w_gate_up.shape[3]
-    )
+    expert_hidden = expert_part(moe_x, expert_ids, expert_weights, w_gate_up)
     return (attn_latent, expert_hidden)
 
 

time: 441 us -> 340 us (0.77)
  waiting for transfers between devices: 329 us -> 142 us
  Pallas kernels: 0 us -> 126 us
  starting transfers between devices: 20.8 us -> 5.21 us
  matrix products: 24.5 us -> 16.4 us
  local copies, waits for them, and re-layouts: 31.7 us -> 25 us
  other arithmetic: 17.1 us -> 10.8 us
    all_to_all x2 -> x0, waiting for transfers between devices: 160 us -> none  [the longest x1 160 us: shards(): lax.all_to_all(outbound, 'dec', split_axis=0, concat_axis=0, tiled=True)]
    pallas_call x0 -> x1, Pallas kernels: none -> 126 us  [expert_part(): pl.pallas_call(expert_kernel, out_shape=jax.ShapeDtypeStruct((EXP_DEV, 25...]
    all_to_all x1, waiting for transfers between devices: 39.3 us -> 0.01 us  [shards(): lax.all_to_all(outgoing, 'dec', split_axis=0, concat_axis=0, tiled=True)]
    all_to_all x2 -> x0, starting transfers between devices: 15.7 us -> none  [the longest x1 10.1 us: shards(): lax.all_to_all(weight_out, 'dec', split_axis=0, concat_axis=0, tiled=True)]
    psum x1, waiting for transfers between devices: 130 us -> 142 us  [shards(): latent_total = lax.psum(partial_sum, 'pre')]
    dot_general x1 -> x0, matrix products: 8.18 us -> none  [shards(): jnp.einsum('secd,etdf->tescf', inbound, w_gate_up, preferred_element_type...]
    gather x1 -> x0, local copies, waits for them, and re-layouts: 7.82 us -> none  [shards(): jnp.take(moe_x, slot_row, axis=0)]
    select_n x2 -> x1, other arithmetic: 7.43 us -> 0.66 us  [expert_part(): jnp.where(c == 0, jnp.concatenate([tag, zero], axis=1), jnp.concatenate([...]
  transfers between devices with their start and end apart: 4 -> 2, of which waited for: 3 -> 1; matrix products, arithmetic and copies ran while one was open for 13% -> 1% of each run, Pallas kernels for 0% -> 37%
where the time goes in v1:
time: 340 us; the launch traced here: 339 us
  waiting for transfers between devices  142 us (42%)
  Pallas kernels  126 us (37%)
  local copies, waits for them, and re-layouts  25 us (7%)
  matrix products  16.4 us (5%)
  between operations  14.2 us (4%)
  other arithmetic  10.8 us (3%)
  starting transfers between devices  5.21 us (2%)
    psum x1, waiting for transfers between devices, shards(): latent_total = lax.psum(partial_sum, 'pre')  142 us
    pallas_call x1, Pallas kernels, expert_part(): pl.pallas_call(expert_kernel, out_shape=jax.ShapeDtypeStruct((EXP_DEV, 25...  126 us
    unnamed x22, local copies, waits for them, and re-layouts  15 us
  transfers between devices with their start and end apart: 2, of which 1 were waited for; matrix products, arithmetic and copies ran while one was open for 1% of the time, Pallas kernels for 37%

profile of v1, /device:TPU:1, one launch (start us, length us, event | category | flops | bytes accessed | tf_op | source)
XLA Modules:
  0.0 339.0 jit_solution(10011893116244708336)
XLA Ops:
  7.2 0.0 copy-start
  7.2 0.0 all-reduce.4.cloned.1.call-start
  7.2 1.2 copy-done
  8.4 3.3 fusion.34
  11.7 0.0 copy-start.6
  11.7 0.0 copy-start.7
  11.7 0.0 all-reduce.4.cloned.1.call-update
  11.7 0.6 copy-done.6
  12.3 0.1 reshape.68
  12.4 0.0 copy-start.3
  12.5 141.8 %all-reduce.4.cloned.1.call-done = f32[1024,576]{0,1:T(8,128)} async-done(((f32[1024,576]{0,1:T(8,128)}), f32[1024,576]{0,1:T(8,128)}) %all-reduce.4.cloned.1.call-update) | async-done | bytes 2359312 | tf_op jit(solution)/shard_map/psum | solution.py:276
  154.2 1.8 multiply_reduce_fusion
  156.0 0.0 copy-done.7
  156.0 1.8 multiply_convert_fusion
  157.8 0.0 copy-done.3
  157.9 1.5 fusion.22
  159.4 0.1 pad_maximum_fusion
  159.5 0.7 copy.23
  160.2 2.4 convert_element_type.39
  162.6 2.0 fusion.2
  164.6 0.5 broadcast.51
  165.1 3.1 reduce
  168.3 4.7 %reshape.73 = bf16[32,2,18432]{2,1,0:T(2,128)(2,1)} reshape(bf16[32,36864]{1,0:T(8,128)(2,1)} %reduce) | data formatting | bytes 4718592
  173.0 0.0 copy-start.2
  173.0 5.2 %all-to-all-start = ((bf16[32,2,18432]{2,1,0:T(2,128)(2,1)}), bf16[32,2,18432]{2,1,0:T(2,128)(2,1)S(1)}, u32[]{:S(2)}, u32[]{:S(2)}) async-start(bf16[32,2,18432]{2,1,0:T(2,128)(2,1)} %reshape.73), calls=%async_computation | async-start | bytes 4718592 | tf_op jit(solution)/shard_map/all_to_all | solution.py:281
  178.2 1.4 reshape.69
  179.5 0.0 copy-done.2
  179.5 0.8 reshape.71
  180.4 0.7 convert_bitcast_fusion
  181.1 0.7 pad_maximum_fusion.1
  181.7 0.7 pad_select_fusion.tag_ref
  182.4 125.7 %shard_map.131 = bf16[4,256,128]{2,1,0:T(8,128)(2,1)} custom-call(bf16[64,4096]{1,0:T(8,128)(2,1)} %moe_hbm.1, bf16[16,128]{1,0:T(8,128)(2,1)} %pad_select_fusion.tag_ref, bf16[4,2,4096,128]{3,2,1,0:T(8,128)(2,1)} %w_hbm.1), custom_call_target="tpu_custom_call" | custom-call | tf_op jit(solution)/shard_map/pallas_call | solution.py:208
  308.1 0.0 copy-done.4
  308.1 0.1 fusion.32
  308.2 0.0 copy-done.5
  308.2 0.1 select_reduce_fusion
  308.3 0.1 fusion.28
  308.5 0.0 copy-done.8
  308.5 0.1 iota_compare_fusion.3
  308.5 0.0 all-to-all-done
  308.5 7.0 %reshape.74 = bf16[32,1,36864]{2,1,0:T(2,128)(2,1)} reshape(bf16[32,2,18432]{2,1,0:T(2,128)(2,1)S(1)} %all-to-all-done) | data formatting | bytes 4718592
  315.5 6.3 %fusion.1 = bf16[32,36864]{1,0:T(8,128)(2,1)S(1)} fusion(bf16[32,36864]{1,0:T(8,128)(2,1)} %param.15, bf16[32,1,36864]{2,1,0:T(2,128)(2,1)} %reshape.74, pred[32]{0:T(512)(128)(4,1)S(1)} %fusion.28, s32[32]{0:T(128)S(1)} %select_reduce_fusion, pred[32]{0:T(512)(128)(4,1)S(1)} %get-tuple-element.2), kind=kOutput, calls=%fused_computation.3 | convolution fusion | flops 77858816 | bytes 7078080 | tf_op jit(solution)/shard_map/dot_general | solution.py:288
  321.9 4.1 %reshape.70 = bf16[8,256,576]{2,1,0:T(8,128)(2,1)} reshape(bf16[32,36864]{1,0:T(8,128)(2,1)S(1)} %fusion.1) | data formatting | bytes 4718592 | tf_op jit(solution)/shard_map/reshape | solution.py:292
  326.0 2.7 fusion.33
  328.7 2.0 fusion.14
  330.7 0.8 copy.28
  331.5 0.0 copy-done.1
  331.5 0.7 copy.36
  (8 shorter events, 0.0 us)
Async XLA Ops:
  7.2 1.2 copy-start
  7.2 147.1 %all-reduce.4.cloned.1.call-start = ((), (), s32[]{:S(2)}) async-start(), calls=%async_computation.1 | async-start | bytes 4718592 | tf_op jit(solution)/shard_map/psum | solution.py:276
  11.7 0.7 copy-start.6
  11.7 144.4 %copy-start.7 = (f32[512]{0:T(512)S(1)}, f32[512]{0:T(512)}, u32[]{:S(2)}) copy-start(f32[512]{0:T(512)} %param.14) | copy-start | bytes 6148
  12.4 145.4 %copy-start.3 = (s32[32,16]{1,0:T(8,128)}, s32[32,16]{1,0:T(8,128)S(1)}, u32[]{:S(2)}) copy-start(s32[32,16]{1,0:T(8,128)S(1)} %reshape.68) | copy-start | bytes 6148
  173.0 6.5 %copy-start.2 = (bf16[8,9216]{1,0:T(8,128)(2,1)S(1)}, bf16[8,9216]{1,0:T(8,128)(2,1)}, u32[]{:S(2)}) copy-start(bf16[8,9216]{1,0:T(8,128)(2,1)} %param.16) | copy-start | bytes 442372
  173.0 135.6 %all-to-all-start = ((bf16[32,2,18432]{2,1,0:T(2,128)(2,1)}), bf16[32,2,18432]{2,1,0:T(2,128)(2,1)S(1)}, u32[]{:S(2)}, u32[]{:S(2)}) async-start(bf16[32,2,18432]{2,1,0:T(2,128)(2,1)} %reshape.73), calls=%async_computation | async-start | bytes 4718592 | tf_op jit(solution)/shard_map/all_to_all | solution.py:281
  182.4 125.7 %copy-start.4 = (s32[32,16]{1,0:T(8,128)S(1)}, s32[32,16]{1,0:T(8,128)}, u32[]{:S(2)}) copy-start(s32[32,16]{1,0:T(8,128)} %copy-done.3) | copy-start | bytes 6148
  182.4 125.8 %copy-start.5 = (s32[32,16]{1,0:T(8,128)S(1)}, s32[32,16]{1,0:T(8,128)}, u32[]{:S(2)}) copy-start(s32[32,16]{1,0:T(8,128)} %reshape.69) | copy-start | bytes 6148
  182.4 126.0 %copy-start.8 = (s32[8]{0:T(128)S(1)}, s32[8]{0:T(128)}, u32[]{:S(2)}) copy-start(s32[8]{0:T(128)} %param.17) | copy-start | bytes 100
  326.0 5.5 %copy-start.1 = (bf16[4,256,128]{2,1,0:T(8,128)(2,1)S(1)}, bf16[4,256,128]{2,1,0:T(8,128)(2,1)}, u32[]{:S(2)}) copy-start(bf16[4,256,128]{2,1,0:T(8,128)(2,1)} %shard_map.131) | copy-start | bytes 786436
Sparse Core Ops, SparseCore 0:
  11.8 142.3 all-reduce.3

commit v2 on v1

v2 whole, which is shorter than its diff:
```python
import jax
import jax.numpy as jnp
import numpy as np
from jax import lax
from jax.experimental import pallas as pl
from jax.experimental.pallas import tpu as pltpu
from jax.sharding import PartitionSpec as P

KVL = 512
LAT = 576
HEAD_QK = 192
PAGE = 64
EXP_DEV = 4
P_TOK = 1024
R_ATT = 8
PAGES_ROW = 4
R_MOE = 64
PP = 16
SLOTS = 32
NORM_EPSILON = 1e-06

MESH = pl.DeviceIdType.MESH
A0, A1, B0, B1 = 0, 1, 2, 3
LEFT = [(-1, 0, A0), (-1, 0, A1), (-1, 0, B0), (-1, 0, B1), (2, 0, A0), (2, 0, B0), (-1, -1, B0), (-1, -1, B1),
        (-1, 1, B0), (-1, 1, B1), (-1, 2, B0), (-1, 2, B1), (2, -1, B0), (2, 1, B0), (2, 2, B0)]
RIGHT = [(1, 0, A1), (1, 0, A0), (1, 0, B1), (1, 0, B0), (2, 0, A1), (2, 0, B1), (1, -1, B1), (1, -1, B0),
         (1, 1, B1), (1, 1, B0), (1, 2, B1), (1, 2, B0), (2, -1, B1), (2, 1, B1), (2, 2, B1)]
BELOW = [(0, -1, B0), (0, -1, B1), (0, -1, A0), (0, -1, A1), (0, 2, B0), (0, 2, A0), (-1, -1, A0), (-1, -1, A1),
         (1, -1, A0), (1, -1, A1), (2, -1, A0), (2, -1, A1), (-1, 2, A0), (1, 2, A0), (2, 2, A0)]
ABOVE = [(0, 1, B1), (0, 1, B0), (0, 1, A1), (0, 1, A0), (0, 2, B1), (0, 2, A1), (-1, 1, A1), (-1, 1, A0),
         (1, 1, A1), (1, 1, A0), (2, 1, A1), (2, 1, A0), (-1, 2, A1), (1, 2, A1), (2, 2, A1)]
def forwards(side, dx, dz, q):
    if side == "left":
        on = [(1, 0)] if dx == -1 and q in (A0, B0) else []
        return on + ([(0, 1), (0, -1)] if q in (A0, A1) else [])
    if side == "right":
        on = [(-1, 0)] if dx == 1 and q in (A1, B1) else []
        return on + ([(0, 1), (0, -1)] if q in (A0, A1) else [])
    if side == "below":
        on = [(0, 1)] if dz == -1 and q in (A0, B0) else []
        return on + ([(1, 0), (-1, 0)] if q in (B0, B1) else [])
    on = [(0, -1)] if dz == 1 and q in (A1, B1) else []
    return on + ([(1, 0), (-1, 0)] if q in (B0, B1) else [])


def device(x, y, z, c):
    return (lax.div(z, 4) * 4 + y, (x * 4 + lax.rem(z, 4)) * 2 + c)


HALVES = 2
HPAGES = PP // HALVES
NEAR = (0, 1, -1, 2)
PASSES = {
    2: [(0, 0)],
    4: [(-1, 0)],
    5: [(1, 0), (0, -1)],
    6: [(0, 1), (2, 0)],
    7: [(0, 2)],
    8: [(-1, -1)],
    10: [(1, -1), (-1, 1), (1, 1)],
    13: [(2, -1), (-1, 2)],
    14: [(2, 1), (1, 2)],
    15: [(2, 2)],
}


def main_kernel(px_hbm, wd_ref, gain_ref, rope_hbm, pool_ref, q_ref, len_ref, dest_ref, slot_in_ref, moe_hbm, tag_ref, w_hbm,
                att_ref, out_ref,
                px, rope, rs_send, rs_recv, acc, zx_send, zx_recv, cache, pg_send, pg_recv, kv_send, kv_recv, kvbuf, q_recv, o_send,
                page_of, slot_of, src_of, rows, tags, wbuf, slot_ref, wt_ref,
                px_sem, rope_sem, rs_ssem, rs_rsem, zx_ssem, zx_rsem, pg_ssem, pg_rsem, kv_ssem, kv_rsem, q_ssem, q_rsem, o_ssem, o_rsem,
                load_sem, w_sem, ici_sem, pair_sem, recv_sem, recv2_sem, tag_send, tag_recv):
    pre, dec = lax.axis_index("pre"), lax.axis_index("dec")
    y = lax.rem(pre, 4)
    c = lax.rem(dec, 2)
    zl = lax.rem(lax.div(dec, 2), 4)
    x = lax.div(dec, 8)
    z = lax.div(pre, 4) * 4 + zl
    features = rows.shape[2]
    quarter = features // 4

    def chip(dx, dz):
        return lax.rem(x + dx + 4, 4) * 4 + lax.rem(z + dz + 8, 4)

    def peer(dx, dz, core):
        return device(lax.rem(x + dx + 4, 4), y, lax.rem(z + dz + 8, 8), core)

    def ypeer(dy):
        return device(x, lax.rem(y + dy, 4), z, c)

    def remote(src, dst, ssem, rsem, where):
        copy = pltpu.make_async_remote_copy(
            src_ref=src, dst_ref=dst, send_sem=ssem, recv_sem=rsem, device_id=where, device_id_type=MESH)
        copy.start()
        return copy

    def landed(ref, sem):
        pltpu.make_async_copy(ref, ref, sem).wait()

    own = pltpu.make_async_copy(moe_hbm, rows.at[chip(0, 0), pl.ds(pl.multiple_of(c * R_MOE, R_MOE), R_MOE)], load_sem)
    own.start()
    px_load = pltpu.make_async_copy(px_hbm, px, px_sem)
    px_load.start()
    rope_load = pltpu.make_async_copy(rope_hbm.at[:, y], rope, rope_sem)
    rope_load.start()
    loads = []
    for e in range(EXP_DEV):
        for t in range(2):
            load = pltpu.make_async_copy(w_hbm.at[e, t], wbuf.at[:, pl.ds((e * 2 + t) * 128, 128)], w_sem.at[e * 2 + t])
            load.start()
            loads.append(load)
    tags[dec] = tag_ref[...]

    barrier = pltpu.get_barrier_semaphore()
    greeted = 0
    for dx in (0, 1, 2, 3):
        for dz in (-2, -1, 0, 1, 2):
            for dc in (0, 1):
                if (dx, dz, dc) != (0, 0, 0):
                    pl.semaphore_signal(barrier, inc=1, device_id=peer(dx, dz, lax.rem(c + dc, 2)), device_id_type=MESH)
                    greeted += 1
    for dy in (1, 2, 3):
        pl.semaphore_signal(barrier, inc=1, device_id=ypeer(dy), device_id_type=MESH)
        greeted += 1
    pl.semaphore_signal(barrier, inc=1, device_id=peer(0, 4, c), device_id_type=MESH)
    greeted += 1
    pl.semaphore_wait(barrier, greeted)

    def piece(dx, dz, q, core):
        return rows.at[chip(dx, dz), pl.ds(pl.multiple_of(core * R_MOE, R_MOE), R_MOE), pl.ds(q * quarter, quarter)]

    def push(dx, dz, q, sx, sz):
        remote(piece(dx, dz, q, c), piece(dx, dz, q, c), ici_sem, recv_sem.at[chip(dx, dz), q], peer(sx, sz, c))

    def share(dx, dz, q):
        remote(piece(dx, dz, q, c), piece(dx, dz, q, c), pair_sem, recv2_sem.at[chip(dx, dz), q], peer(0, 0, 1 - c))

    own.wait()
    for q in (A0, B0, A1, B1):
        push(0, 0, q, 1, 0)
        push(0, 0, (q + 2) % 4, 0, 1)
        push(0, 0, q ^ 1, -1, 0)
        push(0, 0, (q + 2) % 4 ^ 1, 0, -1)

    px_load.wait()
    rs_copies = []
    for h in range(HALVES):
        for dy in (2, 1, 3, 0):
            yy = lax.rem(y + dy, 4)
            lhs = px[pl.ds(h * HPAGES, HPAGES), yy].reshape(HPAGES * 16, px.shape[3])
            part = jnp.dot(lhs, wd_ref[...], preferred_element_type=jnp.float32)
            if dy:
                rs_send[dy - 1, h] = part.astype(jnp.bfloat16)
                rs_copies.append(remote(rs_send.at[dy - 1, h], rs_recv.at[dy - 1, h], rs_ssem.at[dy - 1, h], rs_rsem.at[dy - 1, h], ypeer(dy)))
            else:
                acc[h] = part

    for q in range(4):
        share(0, 0, q)
    tag_copies = []
    for dx in (0, 1, 2, 3):
        for dz in NEAR:
            for dc in (0, 1):
                if (dx, dz, dc) != (0, 0, 0):
                    n = len(tag_copies)
                    tag_copies.append(remote(tag_ref, tags.at[dec], tag_send.at[n], tag_recv.at[dec], peer(dx, dz, lax.rem(c + dc, 2))))
    q_copies = []
    for dy in (1, 2, 3):
        yy = lax.rem(y + dy, 4)
        q_copies.append(remote(q_ref.at[yy], q_recv.at[y], q_ssem.at[dy - 1], q_rsem.at[y], ypeer(dy)))
    q_recv[y] = q_ref[y]

    dests = [dest_ref[dec * PP + p] for p in range(PP)]

    def find_page(d, carry):
        found = jnp.int32(0)
        for p in range(PP):
            found = jnp.where(dests[p] == d, p, found)
        page_of[d] = found
        return carry

    lax.fori_loop(0, 32, find_page, 0)

    def find_slot(s, carry):
        found = jnp.int32(-1)
        for p in range(PP):
            found = jnp.where(dest_ref[s * PP + p] == dec, slot_in_ref[s * PP + p], found)
        slot_of[s] = found
        return carry

    lax.fori_loop(0, 32, find_slot, 0)

    def find_source(k, carry):
        found = jnp.int32(-1)
        for s in range(32):
            found = jnp.where(slot_of[s] == k, s, found)
        src_of[k] = found
        return carry

    lax.fori_loop(0, SLOTS, find_source, 0)

    def read_tags():
        for dx in (0, 1, 2, 3):
            for dz in NEAR:
                for dc in (0, 1):
                    if (dx, dz, dc) != (0, 0, 0):
                        s = 2 * chip(dx, dz) + lax.rem(c + dc, 2)
                        landed(tags.at[s], tag_recv.at[s])
        both = tags[...].astype(jnp.float32).reshape(16, 2, 16, 128)
        both = both[:, 0] + both[:, 1]
        ids, weights = both[:, :8], both[:, 8:]
        i0 = lax.broadcasted_iota(jnp.int32, (128, 128), 0)
        i1 = lax.broadcasted_iota(jnp.int32, (128, 128), 1)
        earlier = ((i0 < i1) & (lax.div(i0, 64) == lax.div(i1, 64))).astype(jnp.float32).astype(jnp.bfloat16)
        shift = jnp.where(lax.broadcasted_iota(jnp.int32, (16, 128), 1) >= 64, 8.0, 0.0)
        for e in range(EXP_DEV):
            hit = ids == (dec * EXP_DEV + e).astype(jnp.float32)
            member = jnp.sum(jnp.where(hit, 1.0, 0.0), axis=1)
            wt_ref[e] = jnp.sum(jnp.where(hit, weights, 0.0), axis=1)
            rank = jnp.dot(member.astype(jnp.bfloat16), earlier, preferred_element_type=jnp.float32)
            slot_ref[e] = jnp.where(member > 0.5, rank + shift, -1.0)

    def wait_item(dx, dz):
        for q in range(4):
            landed(piece(dx, dz, q, 1 - c), recv2_sem.at[chip(dx, dz), q])

    def experts(dx, dz):
        k = chip(dx, dz)
        i0 = lax.broadcasted_iota(jnp.int32, (128, 128), 0)
        i1 = lax.broadcasted_iota(jnp.int32, (128, 128), 1)
        place = lax.broadcasted_iota(jnp.int32, (16, 128), 0).astype(jnp.float32)
        both = jnp.dot(rows[k], wbuf[...], preferred_element_type=jnp.float32)
        for e in range(EXP_DEV):
            gate, up = both[:, e * 256:e * 256 + 128], both[:, e * 256 + 128:e * 256 + 256]
            wrow = wt_ref[e, pl.ds(k, 1), :]
            spread = jnp.where(i0 == i1, jnp.broadcast_to(wrow, (128, 128)), 0.0).astype(jnp.bfloat16)
            wcol = jnp.dot(spread, jnp.ones((128, 128), jnp.bfloat16), preferred_element_type=jnp.float32)
            hidden = (gate / (1.0 + jnp.exp(-gate)) * up * wcol).astype(jnp.bfloat16)
            srow = slot_ref[e, pl.ds(k, 1), :]
            choose = jnp.where(jnp.broadcast_to(srow, (16, 128)) == place, 1.0, 0.0).astype(jnp.bfloat16)
            out_ref[e, pl.ds(pl.multiple_of(k * 16, 16), 16), :] = jnp.dot(
                choose, hidden, preferred_element_type=jnp.float32).astype(jnp.bfloat16)

    zx_copies, pg_copies, kv_copies, o_copies = [], [], [], []

    def add_y(h):
        total = acc[h]
        for dy in (1, 2, 3):
            landed(rs_recv.at[dy - 1, h], rs_rsem.at[dy - 1, h])
            total = total + rs_recv[dy - 1, h].astype(jnp.float32)
        acc[h] = total
        zx_send[h] = total.astype(jnp.bfloat16)
        zx_copies.append(remote(zx_send.at[h], zx_recv.at[h], zx_ssem.at[h], zx_rsem.at[h], peer(0, 4, c)))

    def finish_cache(h):
        landed(zx_recv.at[h], zx_rsem.at[h])
        if h == 0:
            rope_load.wait()
        total = acc[h] + zx_recv[h].astype(jnp.float32)
        lat, turn = total[:, :KVL], total[:, KVL:]
        normed = lat * lax.rsqrt(jnp.mean(lat * lat, axis=1, keepdims=True) + NORM_EPSILON) * gain_ref[...]
        table = rope[pl.ds(h * HPAGES, HPAGES)].reshape(HPAGES * 16, 128)
        swapped = jnp.concatenate([turn[:, 32:], turn[:, :32]], axis=1)
        turned = turn * table[:, :64] + swapped * table[:, 64:]
        done = jnp.concatenate([normed, turned], axis=1).astype(jnp.bfloat16)
        cache[pl.ds(h * HPAGES, HPAGES)] = done.reshape(HPAGES, 16, LAT)

    def send_pages():
        n = 0
        for dx in (0, 1, 2, 3):
            for dz in NEAR:
                for dc in (0, 1):
                    cc = lax.rem(c + dc, 2)
                    page = cache[page_of[2 * chip(dx, dz) + cc]]
                    if (dx, dz, dc) == (0, 0, 0):
                        pg_recv[dec] = page
                        continue
                    pg_send[n] = page
                    pg_copies.append(remote(pg_send.at[n], pg_recv.at[dec], pg_ssem.at[n], pg_rsem.at[dec], peer(dx, dz, cc)))
                    n += 1

    def place_pages():
        for dx in (0, 1, 2, 3):
            for dz in NEAR:
                for dc in (0, 1):
                    if (dx, dz, dc) != (0, 0, 0):
                        s = 2 * chip(dx, dz) + lax.rem(c + dc, 2)
                        landed(pg_recv.at[s], pg_rsem.at[s])
        for k in range(SLOTS):
            kv_send[k // 8, k % 8] = pg_recv[jnp.maximum(src_of[k], 0)]
        for dy in (1, 2, 3):
            yy = lax.rem(y + dy, 4)
            kv_copies.append(remote(kv_send.at[yy], kv_recv.at[y], kv_ssem.at[dy - 1], kv_rsem.at[y], ypeer(dy)))
        kv_recv[y] = kv_send[y]

    def attend():
        for dy in (1, 2, 3):
            yy = lax.rem(y + dy, 4)
            landed(kv_recv.at[yy], kv_rsem.at[yy])
            landed(q_recv.at[yy], q_rsem.at[yy])
        for k in range(8):
            fresh = src_of[y * 8 + k] >= 0
            for yy in range(4):
                kvbuf[k // 4, yy, k % 4] = jnp.where(fresh, kv_recv[yy, k], pool_ref[k, yy])
        col = lax.broadcasted_iota(jnp.int32, (64, 256), 1)
        at = lax.rem(lax.div(col, 16), 4) * PAGE + lax.div(col, 64) * 16 + lax.rem(col, 16)
        for rr in range(2):
            kv = kvbuf[rr].reshape(PAGES_ROW * PAGE, LAT)
            query = q_recv[:, rr].reshape(64, LAT)
            scores = lax.dot_general(query, kv, (((1,), (1,)), ((), ())), preferred_element_type=jnp.float32) * HEAD_QK ** (-0.5)
            masked = jnp.where(at < len_ref[2 * y + rr], scores, -jnp.inf)
            raw = jnp.exp(masked - jnp.max(masked, axis=1, keepdims=True))
            probs = (raw / jnp.sum(raw, axis=1, keepdims=True)).astype(jnp.bfloat16)
            got = jnp.dot(probs, kv[:, :KVL], preferred_element_type=jnp.float32).astype(jnp.bfloat16)
            o_send[:, rr] = got.reshape(4, 16, KVL)
        for dy in (1, 2, 3):
            yy = lax.rem(y + dy, 4)
            o_copies.append(remote(o_send.at[yy], att_ref.at[y], o_ssem.at[dy - 1], o_rsem.at[y], ypeer(dy)))
        att_ref[y] = o_send[y]

    events = {3: [lambda: add_y(0)], 5: [lambda: add_y(1)], 6: [lambda: finish_cache(0)],
              8: [lambda: finish_cache(1), send_pages], 11: [place_pages], 13: [attend]}

    for n in range(1, 16):
        for side, plan in (("left", LEFT), ("right", RIGHT), ("below", BELOW), ("above", ABOVE)):
            dx, dz, q = plan[n - 1]
            landed(piece(dx, dz, q, c), recv_sem.at[chip(dx, dz), q])
            for sx, sz in forwards(side, dx, dz, q):
                push(dx, dz, q, sx, sz)
            share(dx, dz, q)
        if n == 2:
            read_tags()
            for load in loads:
                load.wait()
        for event in events.get(n, []):
            event()
        for dx, dz in PASSES.get(n, []):
            wait_item(dx, dz)
            experts(dx, dz)

    for dy in (1, 2, 3):
        yy = lax.rem(y + dy, 4)
        landed(att_ref.at[yy], o_rsem.at[yy])
    landed(rows.at[pl.ds(0, 8)], pair_sem)
    landed(rows.at[pl.ds(0, 15), pl.ds(0, R_MOE)], ici_sem)
    for copy in tag_copies + q_copies + rs_copies + zx_copies + pg_copies + kv_copies + o_copies:
        copy.wait_send()


def rope_table():
    place = np.arange(P_TOK, dtype=np.float32)[:, None]
    angle = (place * (10000.0 ** (-2.0 * np.arange(32, dtype=np.float64) / 64)).astype(np.float32)[None, :]).astype(np.float64)
    cosine, sine = np.cos(angle), np.sin(angle)
    return np.concatenate([cosine, cosine, -sine, sine], axis=1).astype(np.float32)


def shards(
    prompt_x,
    w_dkv,
    kv_gain,
    cache_pool,
    queries,
    row_lengths,
    page_dest,
    page_slot,
    moe_x,
    expert_ids,
    expert_weights,
    w_gate_up,
):
    dec = lax.axis_index("dec")
    y = lax.rem(lax.axis_index("pre"), 4)
    c = lax.rem(dec, 2)
    tag = jnp.concatenate([expert_ids.T.astype(jnp.bfloat16), expert_weights.T], axis=0)
    zero = jnp.zeros_like(tag)
    tag = jnp.where(c == 0, jnp.concatenate([tag, zero], axis=1), jnp.concatenate([zero, tag], axis=1))
    features = moe_x.shape[1]
    part = prompt_x.shape[1]
    px = prompt_x.reshape(PP, 4, 16, part)
    rope = jnp.asarray(rope_table()).reshape(PP, 4, 16, 128)
    pool = lax.dynamic_slice_in_dim(cache_pool, y * 8, 8, 0).reshape(8, 4, 16, LAT)
    heads = queries.shape[1] // LAT
    q = queries.reshape(4, 2, heads, LAT)
    vmem = pl.BlockSpec(memory_space=pltpu.VMEM)
    smem = pl.BlockSpec(memory_space=pltpu.SMEM)
    hbm = pl.BlockSpec(memory_space=pl.ANY)
    dma = pltpu.SemaphoreType.DMA
    bf = jnp.bfloat16
    att, out = pl.pallas_call(
        main_kernel,
        out_shape=(jax.ShapeDtypeStruct((4, 2, heads, KVL), bf), jax.ShapeDtypeStruct((EXP_DEV, 256, 128), bf)),
        in_specs=[hbm, vmem, vmem, hbm, vmem, vmem, smem, smem, smem, hbm, vmem, hbm],
        out_specs=(vmem, vmem),
        scratch_shapes=[
            pltpu.VMEM((PP, 4, 16, part), bf),
            pltpu.VMEM((PP, 16, 128), jnp.float32),
            pltpu.VMEM((3, HALVES, HPAGES * 16, LAT), bf),
            pltpu.VMEM((3, HALVES, HPAGES * 16, LAT), bf),
            pltpu.VMEM((HALVES, HPAGES * 16, LAT), jnp.float32),
            pltpu.VMEM((HALVES, HPAGES * 16, LAT), bf),
            pltpu.VMEM((HALVES, HPAGES * 16, LAT), bf),
            pltpu.VMEM((PP, 16, LAT), bf),
            pltpu.VMEM((31, 16, LAT), bf),
            pltpu.VMEM((32, 16, LAT), bf),
            pltpu.VMEM((4, 8, 16, LAT), bf),
            pltpu.VMEM((4, 8, 16, LAT), bf),
            pltpu.VMEM((2, 4, 4, 16, LAT), bf),
            pltpu.VMEM((4, 2, heads, LAT), bf),
            pltpu.VMEM((4, 2, heads, KVL), bf),
            pltpu.SMEM((32,), jnp.int32),
            pltpu.SMEM((32,), jnp.int32),
            pltpu.SMEM((32,), jnp.int32),
            pltpu.VMEM((16, 2 * R_MOE, features), bf),
            pltpu.VMEM((32, 16, 128), bf),
            pltpu.VMEM((features, EXP_DEV * 256), bf),
            pltpu.VMEM((EXP_DEV, 16, 128), jnp.float32),
            pltpu.VMEM((EXP_DEV, 16, 128), jnp.float32),
            dma, dma, dma((3, HALVES)), dma((3, HALVES)), dma((HALVES,)), dma((HALVES,)), dma((31,)), dma((32,)),
            dma((3,)), dma((4,)), dma((3,)), dma((4,)), dma((3,)), dma((4,)),
            dma, dma((8,)), dma, dma, dma((16, 4)), dma((16, 4)), dma((31,)), dma((32,)),
        ],
        compiler_params=pltpu.CompilerParams(collective_id=0, has_side_effects=True, vmem_limit_bytes=58 * 1024 * 1024),
    )(px, w_dkv, kv_gain.reshape(1, KVL), rope, pool, q, row_lengths, page_dest, page_slot, moe_x, tag, w_gate_up)
    return (att.reshape(R_ATT, heads * KVL), out)


def solution(mesh):
    return jax.shard_map(
        shards,
        mesh=mesh,
        in_specs=(
            P("dec", "pre"),
            P("pre", None),
            P(),
            P("dec", None),
            P("dec", "pre"),
            P("dec"),
            P(),
            P(),
            P("dec", None),
            P("dec", None),
            P("dec", None),
            P("dec", None, None, "pre"),
        ),
        out_specs=(P("dec", "pre"), P("dec", None, "pre")),
        check_vma=False,
    )
```

time: 340 us -> 116 us (0.34)
  waiting for transfers between devices: 142 us -> 0 us
  Pallas kernels: 126 us -> 105 us
  local copies, waits for them, and re-layouts: 25 us -> 7.83 us
  matrix products: 16.4 us -> 0 us
  between operations: 14.2 us -> 0.68 us
  other arithmetic: 10.8 us -> 2.23 us
  starting transfers between devices: 5.21 us -> 0 us
    psum x1 -> x0, waiting for transfers between devices: 142 us -> none  [shards(): latent_total = lax.psum(partial_sum, 'pre')]
    pallas_call x1, Pallas kernels: 126 us -> 105 us  [shards(): pl.pallas_call(main_kernel, out_shape=(jax.ShapeDtypeStruct((4, 2, heads,...]
    dot_general x4 -> x0, matrix products: 13.6 us -> none  [the longest x1 6.34 us: shards(): jnp.dot(placing.astype(jnp.bfloat16), arrived, preferred_element_type=jnp...]
    unnamed x22 -> x7, local copies, waits for them, and re-layouts: 15 us -> 4.4 us
    all_to_all x1 -> x0, starting transfers between devices: 5.17 us -> none  [shards(): lax.all_to_all(outgoing, 'dec', split_axis=0, concat_axis=0, tiled=True)]
  transfers between devices with their start and end apart: 2 -> 0, of which waited for: 1 -> 0; matrix products, arithmetic and copies ran while one was open for 1% -> 0% of each run, Pallas kernels for 37% -> 0%
where the time goes in v2:
time: 116 us
  Pallas kernels  105 us (91%)
  local copies, waits for them, and re-layouts  7.83 us (7%)
  other arithmetic  2.23 us (2%)
    pallas_call x1, Pallas kernels, shards(): pl.pallas_call(main_kernel, out_shape=(jax.ShapeDtypeStruct((4, 2, heads,...  105 us
    unnamed x7, local copies, waits for them, and re-layouts  4.4 us

profile of v2, /device:TPU:1, one launch (start us, length us, event | category | flops | bytes accessed | tf_op | source)
XLA Modules:
  0.0 116.2 jit_solution(2736985753062475613)
XLA Ops:
  0.6 0.0 copy-start
  0.6 0.0 copy-start.1
  0.7 0.8 convert_bitcast_fusion
  1.5 0.7 pad_maximum_fusion
  2.2 0.7 pad_select_fusion.tag_ref
  2.9 1.7 %reshape.26.q_ref = bf16[4,2,16,576]{3,2,1,0:T(8,128)(2,1)} reshape(bf16[8,9216]{1,0:T(8,128)(2,1)} %param.17) | data formatting | bytes 294912 | tf_op jit(solution)/shard_map/reshape | solution.py:383
  4.6 0.0 copy-done
  4.7 1.6 %reshape.25.pool_ref = bf16[8,4,16,576]{3,2,1,0:T(8,128)(2,1)} reshape(bf16[8,36864]{1,0:T(8,128)(2,1)S(1)} %constant_dynamic-slice_fusion) | data formatting | bytes 1179648 | tf_op jit(solution)/shard_map/reshape | solution.py:381
  6.3 0.0 copy-done.1
  6.3 1.1 copy.15.wd_ref
  7.4 105.5 %shard_map.140 = (bf16[4,2,16,512]{3,2,1,0:T(8,128)(2,1)}, bf16[4,256,128]{2,1,0:T(8,128)(2,1)}) custom-call(bf16[16,4,16,512]{3,2,1,0:T(8,128)(2,1)} %bitcast.8, bf16[512,576]{1,0:T(8,128)(2,1)} %copy.15.wd_ref, f32[1,512]{1,0:T(1,128)} %bitcast.11, f32[16,4,16,128]{3,2,1,0:T(8,128)} %constant.35.rope_hbm, bf16[8,4,16,576]{3,2,1,0:T(8,128)(2,1)} %reshape.25.pool_ref, ...), custom_call_target="tpu_custom_call" | custom-call | tf_op jit(solution)/shard_map/pallas_call | solution.py:389
  112.9 1.6 %copy.16 = bf16[1,8,16,512]{3,1,2,0:T(8,128)(2,1)} copy(bf16[1,8,16,512]{3,2,1,0:T(8,128)(2,1)} %bitcast.10) | data formatting | bytes 262144
  114.6 1.7 %copy.18 = bf16[4,256,128]{2,1,0:T(8,128)(2,1)} copy(bf16[4,256,128]{2,1,0:T(8,128)(2,1)} %get-tuple-element.9) | data formatting | bytes 524288
  (1 shorter events, 0.0 us)
Async XLA Ops:
  0.6 4.0 %copy-start = (bf16[32,36864]{1,0:T(8,128)(2,1)S(1)}, bf16[32,36864]{1,0:T(8,128)(2,1)}, u32[]{:S(2)}) copy-start(bf16[32,36864]{1,0:T(8,128)(2,1)} %param.16) | copy-start | bytes 7077892
  0.6 5.7 %copy-start.1 = (bf16[512,576]{0,1:T(8,128)(2,1)S(1)}, bf16[512,576]{0,1:T(8,128)(2,1)}, u32[]{:S(2)}) copy-start(bf16[512,576]{0,1:T(8,128)(2,1)} %param.14) | copy-start | bytes 1769476

commit v3 on v2

--- a/solution.py
+++ b/solution.py
@@ -29,20 +29,6 @@
          (1, -1, A0), (1, -1, A1), (2, -1, A0), (2, -1, A1), (-1, 2, A0), (1, 2, A0), (2, 2, A0)]
 ABOVE = [(0, 1, B1), (0, 1, B0), (0, 1, A1), (0, 1, A0), (0, 2, B1), (0, 2, A1), (-1, 1, A1), (-1, 1, A0),
          (1, 1, A1), (1, 1, A0), (2, 1, A1), (2, 1, A0), (-1, 2, A1), (1, 2, A1), (2, 2, A1)]
-def forwards(side, dx, dz, q):
-    if side == "left":
-        on = [(1, 0)] if dx == -1 and q in (A0, B0) else []
-        return on + ([(0, 1), (0, -1)] if q in (A0, A1) else [])
-    if side == "right":
-        on = [(-1, 0)] if dx == 1 and q in (A1, B1) else []
-        return on + ([(0, 1), (0, -1)] if q in (A0, A1) else [])
-    if side == "below":
-        on = [(0, 1)] if dz == -1 and q in (A0, B0) else []
-        return on + ([(1, 0), (-1, 0)] if q in (B0, B1) else [])
-    on = [(0, -1)] if dz == 1 and q in (A1, B1) else []
-    return on + ([(1, 0), (-1, 0)] if q in (B0, B1) else [])
-
-
 def device(x, y, z, c):
     return (lax.div(z, 4) * 4 + y, (x * 4 + lax.rem(z, 4)) * 2 + c)
 
@@ -50,25 +36,29 @@
 HALVES = 2
 HPAGES = PP // HALVES
 NEAR = (0, 1, -1, 2)
-PASSES = {
-    2: [(0, 0)],
-    4: [(-1, 0)],
-    5: [(1, 0), (0, -1)],
-    6: [(0, 1), (2, 0)],
-    7: [(0, 2)],
-    8: [(-1, -1)],
-    10: [(1, -1), (-1, 1), (1, 1)],
-    13: [(2, -1), (-1, 2)],
-    14: [(2, 1), (1, 2)],
-    15: [(2, 2)],
-}
-
-
-def main_kernel(px_hbm, wd_ref, gain_ref, rope_hbm, pool_ref, q_ref, len_ref, dest_ref, slot_in_ref, moe_hbm, tag_ref, w_hbm,
+COLS = {A0: (0, 512), A1: (512, 512), B0: (1024, 1152), B1: (2176, 1152)}
+A_END, STRIP, AB_END = 1024, 2048, 3328
+FIRST = {2: [(0, 0)], 4: [(-1, 0), (1, 0)], 5: [(0, -1), (0, 1)], 6: [(2, 0)], 7: [(0, 2)], 8: [(-1, -1)],
+         10: [(1, -1), (-1, 1)], 11: [(1, 1)], 13: [(2, -1), (-1, 2)], 14: [(2, 1), (1, 2)], 15: [(2, 2)]}
+FINISH = {2: [(0, 0)], 6: [(0, -1), (0, 1)], 8: [(-1, 0), (1, 0)], 9: [(0, 2), (2, 0)], 11: [(-1, -1)], 12: [(1, -1)],
+          13: [(-1, 1), (1, 1)], 15: [(-1, 2), (1, 2)], 16: [(2, -1), (2, 1), (2, 2)]}
+A_DONE = {2: [(-1, 0), (1, 0)], 4: [(0, -1), (0, 1)], 5: [(2, 0)], 6: [(0, 2)], 8: [(-1, -1), (-1, 1)], 10: [(1, -1), (1, 1)],
+          12: [(2, -1), (2, 1)], 13: [(-1, 2)], 14: [(1, 2)], 15: [(2, 2)]}
+B_DONE = {2: [(0, -1), (0, 1)], 4: [(-1, 0), (1, 0)], 5: [(0, 2)], 6: [(2, 0)], 8: [(-1, -1), (1, -1)], 10: [(-1, 1), (1, 1)],
+          12: [(-1, 2), (1, 2)], 13: [(2, -1)], 14: [(2, 1)], 15: [(2, 2)]}
+STRIPS = {4: [(0, -1), (0, 1)], 6: [(-1, 0), (1, 0)], 7: [(0, 2)], 8: [(2, 0)], 10: [(-1, -1), (1, -1)], 12: [(-1, 1), (1, 1)],
+          14: [(-1, 2), (1, 2)], 15: [(2, -1)], 16: [(2, 1), (2, 2)]}
+NEXT = {0: (1, 2, 3, 4), 1: (5,), 3: (6, 7), 4: (8,), 5: (9, 10), 6: (11,), 7: (12,), 8: (13,), 9: (14,), 11: (15,)}
+HALVES = 2
+HPAGES = PP // HALVES
+NEAR = (0, 1, -1, 2)
+
+
+def main_kernel(px_hbm, wd_hbm, gain_ref, rope_hbm, pool_ref, q_ref, len_ref, dest_ref, slot_in_ref, moe_hbm, ids_ref, ew_ref, w_hbm,
                 att_ref, out_ref,
-                px, rope, rs_send, rs_recv, acc, zx_send, zx_recv, cache, pg_send, pg_recv, kv_send, kv_recv, kvbuf, q_recv, o_send,
+                px, wd_ref, tag_ref, esum, rope, rs_send, rs_recv, acc, zx_send, zx_recv, cache, pg_send, pg_recv, kv_send, kv_recv, kvbuf, q_recv, o_send,
                 page_of, slot_of, src_of, rows, tags, wbuf, slot_ref, wt_ref,
-                px_sem, rope_sem, rs_ssem, rs_rsem, zx_ssem, zx_rsem, pg_ssem, pg_rsem, kv_ssem, kv_rsem, q_ssem, q_rsem, o_ssem, o_rsem,
+                px_sem, wd_sem, strip_ssem, strip_rsem, rope_sem, rs_ssem, rs_rsem, zx_ssem, zx_rsem, pg_ssem, pg_rsem, kv_ssem, kv_rsem, q_ssem, q_rsem, o_ssem, o_rsem,
                 load_sem, w_sem, ici_sem, pair_sem, recv_sem, recv2_sem, tag_send, tag_recv):
     pre, dec = lax.axis_index("pre"), lax.axis_index("dec")
     y = lax.rem(pre, 4)
@@ -77,7 +67,6 @@
     x = lax.div(dec, 8)
     z = lax.div(pre, 4) * 4 + zl
     features = rows.shape[2]
-    quarter = features // 4
 
     def chip(dx, dz):
         return lax.rem(x + dx + 4, 4) * 4 + lax.rem(z + dz + 8, 4)
@@ -97,20 +86,18 @@
     def landed(ref, sem):
         pltpu.make_async_copy(ref, ref, sem).wait()
 
-    own = pltpu.make_async_copy(moe_hbm, rows.at[chip(0, 0), pl.ds(pl.multiple_of(c * R_MOE, R_MOE), R_MOE)], load_sem)
-    own.start()
+    def strip_from(dy):
+        return pl.multiple_of(A_END * 3 + lax.rem(y - dy + 4, 4) * 256, 256)
+
+    chunks = [(0, 0, 2048), (STRIP, strip_from(0), 256), (STRIP + 256, 2048, 1024)]
+    chunks += [(AB_END + 256 * (dy - 1), strip_from(dy), 256) for dy in (1, 2, 3)]
+    mine = pl.ds(pl.multiple_of(c * R_MOE, R_MOE), R_MOE)
     px_load = pltpu.make_async_copy(px_hbm, px, px_sem)
     px_load.start()
-    rope_load = pltpu.make_async_copy(rope_hbm.at[:, y], rope, rope_sem)
-    rope_load.start()
-    loads = []
-    for e in range(EXP_DEV):
-        for t in range(2):
-            load = pltpu.make_async_copy(w_hbm.at[e, t], wbuf.at[:, pl.ds((e * 2 + t) * 128, 128)], w_sem.at[e * 2 + t])
-            load.start()
-            loads.append(load)
-    tags[dec] = tag_ref[...]
-
+    wd_load = pltpu.make_async_copy(wd_hbm, wd_ref, wd_sem)
+    wd_load.start()
+    for to, of, size in chunks:
+        pltpu.make_async_copy(moe_hbm.at[:, pl.ds(of, size)], rows.at[chip(0, 0), mine, pl.ds(to, size)], load_sem).start()
     barrier = pltpu.get_barrier_semaphore()
     greeted = 0
     for dx in (0, 1, 2, 3):
@@ -124,39 +111,83 @@
         greeted += 1
     pl.semaphore_signal(barrier, inc=1, device_id=peer(0, 4, c), device_id_type=MESH)
     greeted += 1
-    pl.semaphore_wait(barrier, greeted)
-
-    def piece(dx, dz, q, core):
-        return rows.at[chip(dx, dz), pl.ds(pl.multiple_of(core * R_MOE, R_MOE), R_MOE), pl.ds(q * quarter, quarter)]
-
-    def push(dx, dz, q, sx, sz):
-        remote(piece(dx, dz, q, c), piece(dx, dz, q, c), ici_sem, recv_sem.at[chip(dx, dz), q], peer(sx, sz, c))
-
-    def share(dx, dz, q):
-        remote(piece(dx, dz, q, c), piece(dx, dz, q, c), pair_sem, recv2_sem.at[chip(dx, dz), q], peer(0, 0, 1 - c))
-
-    own.wait()
-    for q in (A0, B0, A1, B1):
-        push(0, 0, q, 1, 0)
-        push(0, 0, (q + 2) % 4, 0, 1)
-        push(0, 0, q ^ 1, -1, 0)
-        push(0, 0, (q + 2) % 4 ^ 1, 0, -1)
+
+    rope_load = pltpu.make_async_copy(rope_hbm.at[:, y], rope, rope_sem)
+    rope_load.start()
+    for e in range(EXP_DEV):
+        for t in range(2):
+            for to, of, size in chunks:
+                pltpu.make_async_copy(
+                    w_hbm.at[e, t, pl.ds(of, size)], wbuf.at[pl.ds(to, size), pl.ds((e * 2 + t) * 128, 128)], w_sem.at[e * 2 + t]).start()
+    i0 = lax.broadcasted_iota(jnp.int32, (R_MOE, 128), 0)
+    i1 = lax.broadcasted_iota(jnp.int32, (R_MOE, 128), 1)
+    spread_rows = jnp.where(i1 == i0 + c * R_MOE, 1.0, 0.0).astype(jnp.bfloat16)
+    tag_rows = [
+        jnp.dot(part, spread_rows, preferred_element_type=jnp.float32)
+        for part in (ids_ref[...].astype(jnp.float32).astype(jnp.bfloat16), ew_ref[...])
+    ]
+    tag_ref[...] = jnp.concatenate(tag_rows, axis=0).astype(jnp.bfloat16)
+    tags[dec] = tag_ref[...]
 
     px_load.wait()
-    rs_copies = []
+    wd_load.wait()
     for h in range(HALVES):
         for dy in (2, 1, 3, 0):
             yy = lax.rem(y + dy, 4)
             lhs = px[pl.ds(h * HPAGES, HPAGES), yy].reshape(HPAGES * 16, px.shape[3])
-            part = jnp.dot(lhs, wd_ref[...], preferred_element_type=jnp.float32)
+            part = lax.dot_general(lhs, wd_ref[...], (((1,), (1,)), ((), ())), preferred_element_type=jnp.float32)
             if dy:
                 rs_send[dy - 1, h] = part.astype(jnp.bfloat16)
-                rs_copies.append(remote(rs_send.at[dy - 1, h], rs_recv.at[dy - 1, h], rs_ssem.at[dy - 1, h], rs_rsem.at[dy - 1, h], ypeer(dy)))
             else:
                 acc[h] = part
-
-    for q in range(4):
-        share(0, 0, q)
+    pl.semaphore_wait(barrier, greeted)
+    rs_copies = []
+    for h in range(HALVES):
+        for dy in (2, 1, 3):
+            rs_copies.append(remote(rs_send.at[dy - 1, h], rs_recv.at[dy - 1, h], rs_ssem.at[dy - 1, h], rs_rsem.at[dy - 1, h], ypeer(dy)))
+
+    def block(dx, dz, core, first, size):
+        return rows.at[chip(dx, dz), pl.ds(pl.multiple_of(core * R_MOE, R_MOE), R_MOE), pl.ds(first, size)]
+
+    def push(dx, dz, q, sx, sz):
+        part = block(dx, dz, c, *COLS[q])
+        remote(part, part, ici_sem, recv_sem.at[chip(dx, dz), q], peer(sx, sz, c))
+
+    def push_next(step):
+        for n in NEXT.get(step, ()):
+            dx, dz, q = LEFT[n - 1]
+            push(dx + 1, dz, q, 1, 0)
+            dx, dz, q = BELOW[n - 1]
+            push(dx, dz + 1, q, 0, 1)
+            dx, dz, q = RIGHT[n - 1]
+            push(dx - 1, dz, q, -1, 0)
+            dx, dz, q = ABOVE[n - 1]
+            push(dx, dz - 1, q, 0, -1)
+
+    SPANS = [(0, A_END), (A_END, AB_END - A_END), (AB_END, features - AB_END)]
+
+    def share(dx, dz, span):
+        part = block(dx, dz, c, *SPANS[span])
+        remote(part, part, pair_sem, recv2_sem.at[chip(dx, dz), span], peer(0, 0, 1 - c))
+
+    def shared(dx, dz, span):
+        landed(block(dx, dz, 1 - c, *SPANS[span]), recv2_sem.at[chip(dx, dz), span])
+
+    def send_strips(dx, dz):
+        for dy in (1, 2, 3):
+            remote(block(dx, dz, c, STRIP, 256), block(dx, dz, c, AB_END + 256 * (dy - 1), 256), strip_ssem,
+                   strip_rsem.at[chip(dx, dz), dy - 1], ypeer(dy))
+
+    def wait_strips(dx, dz):
+        for dy in (1, 2, 3):
+            landed(block(dx, dz, c, AB_END + 256 * (dy - 1), 256), strip_rsem.at[chip(dx, dz), dy - 1])
+        share(dx, dz, 2)
+
+    landed(block(0, 0, c, 0, features), load_sem)
+    push_next(0)
+
+    for span in range(3):
+        share(0, 0, span)
     tag_copies = []
     for dx in (0, 1, 2, 3):
         for dz in NEAR:
@@ -170,34 +201,36 @@
         q_copies.append(remote(q_ref.at[yy], q_recv.at[y], q_ssem.at[dy - 1], q_rsem.at[y], ypeer(dy)))
     q_recv[y] = q_ref[y]
 
-    dests = [dest_ref[dec * PP + p] for p in range(PP)]
-
-    def find_page(d, carry):
-        found = jnp.int32(0)
-        for p in range(PP):
-            found = jnp.where(dests[p] == d, p, found)
-        page_of[d] = found
-        return carry
-
-    lax.fori_loop(0, 32, find_page, 0)
-
-    def find_slot(s, carry):
-        found = jnp.int32(-1)
-        for p in range(PP):
-            found = jnp.where(dest_ref[s * PP + p] == dec, slot_in_ref[s * PP + p], found)
-        slot_of[s] = found
-        return carry
-
-    lax.fori_loop(0, 32, find_slot, 0)
-
-    def find_source(k, carry):
-        found = jnp.int32(-1)
-        for s in range(32):
-            found = jnp.where(slot_of[s] == k, s, found)
-        src_of[k] = found
-        return carry
-
-    lax.fori_loop(0, SLOTS, find_source, 0)
+    def read_tables():
+        dests = [dest_ref[dec * PP + p] for p in range(PP)]
+
+        def find_page(d, carry):
+            found = jnp.int32(0)
+            for p in range(PP):
+                found = jnp.where(dests[p] == d, p, found)
+            page_of[d] = found
+            return carry
+
+        lax.fori_loop(0, 32, find_page, 0)
+
+        def find_slot(s, carry):
+            found = jnp.int32(-1)
+            for p in range(PP):
+                found = jnp.where(dest_ref[s * PP + p] == dec, slot_in_ref[s * PP + p], found)
+            slot_of[s] = found
+            return carry
+
+        lax.fori_loop(0, 32, find_slot, 0)
+
+        def find_source(k, carry):
+            found = jnp.int32(-1)
+            for s in range(32):
+                found = jnp.where(slot_of[s] == k, s, found)
+            src_of[k] = found
+            return carry
+
+        lax.fori_loop(0, SLOTS, find_source, 0)
+
 
     def read_tags():
         for dx in (0, 1, 2, 3):
@@ -220,16 +253,19 @@
             rank = jnp.dot(member.astype(jnp.bfloat16), earlier, preferred_element_type=jnp.float32)
             slot_ref[e] = jnp.where(member > 0.5, rank + shift, -1.0)
 
-    def wait_item(dx, dz):
-        for q in range(4):
-            landed(piece(dx, dz, q, 1 - c), recv2_sem.at[chip(dx, dz), q])
-
-    def experts(dx, dz):
+    def first_product(dx, dz):
+        shared(dx, dz, 0)
+        shared(dx, dz, 1)
+        k = chip(dx, dz)
+        esum[k] = jnp.dot(rows[k, :, :AB_END], wbuf[:AB_END], preferred_element_type=jnp.float32)
+
+    def finish_product(dx, dz):
+        shared(dx, dz, 2)
         k = chip(dx, dz)
         i0 = lax.broadcasted_iota(jnp.int32, (128, 128), 0)
         i1 = lax.broadcasted_iota(jnp.int32, (128, 128), 1)
         place = lax.broadcasted_iota(jnp.int32, (16, 128), 0).astype(jnp.float32)
-        both = jnp.dot(rows[k], wbuf[...], preferred_element_type=jnp.float32)
+        both = esum[k] + jnp.dot(rows[k, :, AB_END:], wbuf[AB_END:], preferred_element_type=jnp.float32)
         for e in range(EXP_DEV):
             gate, up = both[:, e * 256:e * 256 + 128], both[:, e * 256 + 128:e * 256 + 256]
             wrow = wt_ref[e, pl.ds(k, 1), :]
@@ -318,31 +354,39 @@
             o_copies.append(remote(o_send.at[yy], att_ref.at[y], o_ssem.at[dy - 1], o_rsem.at[y], ypeer(dy)))
         att_ref[y] = o_send[y]
 
-    events = {3: [lambda: add_y(0)], 5: [lambda: add_y(1)], 6: [lambda: finish_cache(0)],
-              8: [lambda: finish_cache(1), send_pages], 11: [place_pages], 13: [attend]}
-
-    for n in range(1, 16):
-        for side, plan in (("left", LEFT), ("right", RIGHT), ("below", BELOW), ("above", ABOVE)):
-            dx, dz, q = plan[n - 1]
-            landed(piece(dx, dz, q, c), recv_sem.at[chip(dx, dz), q])
-            for sx, sz in forwards(side, dx, dz, q):
-                push(dx, dz, q, sx, sz)
-            share(dx, dz, q)
+    events = {1: [read_tables], 2: [lambda: add_y(0)], 4: [lambda: add_y(1)], 5: [lambda: finish_cache(0)],
+              7: [lambda: finish_cache(1), send_pages], 11: [place_pages], 15: [attend]}
+
+    for n in range(1, 17):
+        if n <= 15:
+            for plan in (LEFT, RIGHT, BELOW, ABOVE):
+                dx, dz, q = plan[n - 1]
+                landed(block(dx, dz, c, *COLS[q]), recv_sem.at[chip(dx, dz), q])
+            push_next(n)
+        for item in B_DONE.get(n, []):
+            send_strips(*item)
+            share(*item, 1)
+        for item in A_DONE.get(n, []):
+            share(*item, 0)
+        for item in STRIPS.get(n, []):
+            wait_strips(*item)
         if n == 2:
             read_tags()
-            for load in loads:
-                load.wait()
+            for i in range(2 * EXP_DEV):
+                landed(wbuf.at[:, pl.ds(i * 128, 128)], w_sem.at[i])
         for event in events.get(n, []):
             event()
-        for dx, dz in PASSES.get(n, []):
-            wait_item(dx, dz)
-            experts(dx, dz)
+        for item in FIRST.get(n, []):
+            first_product(*item)
+        for item in FINISH.get(n, []):
+            finish_product(*item)
 
     for dy in (1, 2, 3):
         yy = lax.rem(y + dy, 4)
         landed(att_ref.at[yy], o_rsem.at[yy])
     landed(rows.at[pl.ds(0, 8)], pair_sem)
-    landed(rows.at[pl.ds(0, 15), pl.ds(0, R_MOE)], ici_sem)
+    landed(rows.at[pl.ds(0, 15), pl.ds(0, R_MOE), pl.ds(0, AB_END)], ici_sem)
+    landed(rows.at[pl.ds(0, 15), pl.ds(0, R_MOE), pl.ds(AB_END, features - AB_END)], strip_ssem)
     for copy in tag_copies + q_copies + rs_copies + zx_copies + pg_copies + kv_copies + o_copies:
         copy.wait_send()
 
@@ -368,12 +412,7 @@
     expert_weights,
     w_gate_up,
 ):
-    dec = lax.axis_index("dec")
     y = lax.rem(lax.axis_index("pre"), 4)
-    c = lax.rem(dec, 2)
-    tag = jnp.concatenate([expert_ids.T.astype(jnp.bfloat16), expert_weights.T], axis=0)
-    zero = jnp.zeros_like(tag)
-    tag = jnp.where(c == 0, jnp.concatenate([tag, zero], axis=1), jnp.concatenate([zero, tag], axis=1))
     features = moe_x.shape[1]
     part = prompt_x.shape[1]
     px = prompt_x.reshape(PP, 4, 16, part)
@@ -389,10 +428,13 @@
     att, out = pl.pallas_call(
         main_kernel,
         out_shape=(jax.ShapeDtypeStruct((4, 2, heads, KVL), bf), jax.ShapeDtypeStruct((EXP_DEV, 256, 128), bf)),
-        in_specs=[hbm, vmem, vmem, hbm, vmem, vmem, smem, smem, smem, hbm, vmem, hbm],
+        in_specs=[hbm, hbm, vmem, hbm, vmem, vmem, smem, smem, smem, hbm, vmem, vmem, hbm],
         out_specs=(vmem, vmem),
         scratch_shapes=[
             pltpu.VMEM((PP, 4, 16, part), bf),
+            pltpu.VMEM((LAT, part), bf),
+            pltpu.VMEM((16, 128), bf),
+            pltpu.VMEM((16, 2 * R_MOE, EXP_DEV * 256), jnp.float32),
             pltpu.VMEM((PP, 16, 128), jnp.float32),
             pltpu.VMEM((3, HALVES, HPAGES * 16, LAT), bf),
             pltpu.VMEM((3, HALVES, HPAGES * 16, LAT), bf),
@@ -415,12 +457,12 @@
             pltpu.VMEM((features, EXP_DEV * 256), bf),
             pltpu.VMEM((EXP_DEV, 16, 128), jnp.float32),
             pltpu.VMEM((EXP_DEV, 16, 128), jnp.float32),
-            dma, dma, dma((3, HALVES)), dma((3, HALVES)), dma((HALVES,)), dma((HALVES,)), dma((31,)), dma((32,)),
+            dma, dma, dma, dma((16, 3)), dma, dma((3, HALVES)), dma((3, HALVES)), dma((HALVES,)), dma((HALVES,)), dma((31,)), dma((32,)),
             dma((3,)), dma((4,)), dma((3,)), dma((4,)), dma((3,)), dma((4,)),
-            dma, dma((8,)), dma, dma, dma((16, 4)), dma((16, 4)), dma((31,)), dma((32,)),
+            dma, dma((8,)), dma, dma, dma((16, 4)), dma((16, 3)), dma((31,)), dma((32,)),
         ],
         compiler_params=pltpu.CompilerParams(collective_id=0, has_side_effects=True, vmem_limit_bytes=58 * 1024 * 1024),
-    )(px, w_dkv, kv_gain.reshape(1, KVL), rope, pool, q, row_lengths, page_dest, page_slot, moe_x, tag, w_gate_up)
+    )(px, w_dkv.T, kv_gain.reshape(1, KVL), rope, pool, q, row_lengths, page_dest, page_slot, moe_x, expert_ids.T, expert_weights.T, w_gate_up)
     return (att.reshape(R_ATT, heads * KVL), out)
 
 

time: 116 us -> 97.5 us (0.84)
  Pallas kernels: 105 us -> 89.2 us
  other arithmetic: 2.23 us -> 0 us
    pallas_call x1, Pallas kernels: 105 us -> 89.2 us  [shards(): pl.pallas_call(main_kernel, out_shape=(jax.ShapeDtypeStruct((4, 2, heads,...]
    unnamed x7 -> x6, local copies, waits for them, and re-layouts: 4.4 us -> 4.95 us
where the time goes in v3:
time: 97.5 us; the launch traced here: 97.4 us
  Pallas kernels  89.2 us (91%)
  local copies, waits for them, and re-layouts  7.47 us (8%)
    pallas_call x1, Pallas kernels, shards(): pl.pallas_call(main_kernel, out_shape=(jax.ShapeDtypeStruct((4, 2, heads,...  89.2 us
    unnamed x6, local copies, waits for them, and re-layouts  4.95 us

profile of v3, /device:TPU:1, one launch (start us, length us, event | category | flops | bytes accessed | tf_op | source)
XLA Modules:
  0.0 97.4 jit_solution(8246116742708920253)
XLA Ops:
  0.6 0.0 copy-start
  0.6 0.0 copy-start.1
  0.7 1.6 %copy-done = bf16[32,36864]{1,0:T(8,128)(2,1)S(1)} copy-done((bf16[32,36864]{1,0:T(8,128)(2,1)S(1)}, bf16[32,36864]{1,0:T(8,128)(2,1)}, u32[]{:S(2)}) %copy-start) | copy-done | bytes 2359320
  2.3 1.6 %reshape.25.pool_ref = bf16[8,4,16,576]{3,2,1,0:T(8,128)(2,1)} reshape(bf16[8,36864]{1,0:T(8,128)(2,1)S(1)} %constant_dynamic-slice_fusion) | data formatting | bytes 1179648 | tf_op jit(solution)/shard_map/reshape | solution.py:420
  4.0 0.0 copy-done.1
  4.0 0.8 reshape.26.q_ref
  4.8 89.2 %shard_map.140 = (bf16[4,2,16,512]{3,2,1,0:T(8,128)(2,1)}, bf16[4,256,128]{2,1,0:T(8,128)(2,1)}) custom-call(bf16[16,4,16,512]{3,2,1,0:T(8,128)(2,1)} %bitcast.8, bf16[576,512]{1,0:T(8,128)(2,1)} %bitcast.9, f32[1,512]{1,0:T(1,128)} %bitcast.13, f32[16,4,16,128]{3,2,1,0:T(8,128)} %constant.22.rope_hbm, bf16[8,4,16,576]{3,2,1,0:T(8,128)(2,1)} %reshape.25.pool_ref, ...), custom_call_target="tpu_custom_call" | custom-call | tf_op jit(solution)/shard_map/pallas_call | solution.py:428
  94.0 1.6 %copy.15 = bf16[1,8,16,512]{3,1,2,0:T(8,128)(2,1)} copy(bf16[1,8,16,512]{3,2,1,0:T(8,128)(2,1)} %bitcast.11) | data formatting | bytes 262144
  95.7 1.7 %copy.17 = bf16[4,256,128]{2,1,0:T(8,128)(2,1)} copy(bf16[4,256,128]{2,1,0:T(8,128)(2,1)} %get-tuple-element.9) | data formatting | bytes 524288
  (1 shorter events, 0.0 us)
Async XLA Ops:
  0.6 1.7 %copy-start = (bf16[32,36864]{1,0:T(8,128)(2,1)S(1)}, bf16[32,36864]{1,0:T(8,128)(2,1)}, u32[]{:S(2)}) copy-start(bf16[32,36864]{1,0:T(8,128)(2,1)} %param.16) | copy-start | bytes 7077892
  0.6 3.3 %copy-start.1 = (bf16[8,9216]{1,0:T(8,128)(2,1)S(1)}, bf16[8,9216]{1,0:T(8,128)(2,1)}, u32[]{:S(2)}) copy-start(bf16[8,9216]{1,0:T(8,128)(2,1)} %param.17) | copy-start | bytes 442372
